TPU v7x, 512 devices: a whole 4x4x16 slice. The times are simulated.
512 devices in a mesh: dp: 64 (over z_lo, y, core), tensor: 8 (over z_hi, x).
Axes of the slice: x: 4, y: 4, z: 16 (z_hi: 2, z_lo: 8; z = z_hi * 8 + z_lo), core: 2. Of those that a mesh axis runs over, the one named last changes fastest.
Arguments:
- activation: bfloat16 [24576, 6656], P('dp', 'tensor'), may hold values from -6 to 6
- w_query: bfloat16 [6656, 1024], P(None, 'tensor'), may hold values from -0.5 to 0.5
- key_rows: bfloat16 [24576, 1024], P('dp', 'tensor'), may hold values from -8 to 8
- value_rows: bfloat16 [24576, 1024], P('dp', 'tensor'), may hold values from -6 to 6
- out_grad: bfloat16 [24576, 1024], P('dp', 'tensor'), may hold values from -6 to 6
- owners: int32 [8, 52, 1], P('tensor'), may hold values from 0 to 63; in each aligned block of 52 rows (0 to 51, 52 to 103, ..., all dimensions but the last counted through in order) at most 2 rows name the same one
- master_copy: float32 [128, 128, 1024], P('dp', None, 'tensor'), may hold values from -0.078125 to 0.078125
- first_moment: float32 [128, 128, 1024], P('dp', None, 'tensor'), may hold values from -4 to 4
- second_moment: float32 [128, 128, 1024], P('dp', None, 'tensor'), may hold values from 0.01 to 1
Outputs:
- new_weights: bfloat16 [6656, 1024], P(None, 'tensor')
- new_master: float32 [128, 128, 1024], P('dp', None, 'tensor')
- new_first: float32 [128, 128, 1024], P('dp', None, 'tensor')
- new_second: float32 [128, 128, 1024], P('dp', None, 'tensor')
Inputs may be any that keep to these rules, and one draw needn't show every extreme that they name: `owners`: within one head no dp index owns more than 2 blocks, one owns exactly 2; every dp index owns some block of some head.
All inputs are finite; a program needn't handle non-finite values.
Results may differ from a plain program's by a relative error of at most 0.0055.
The roundings to bfloat16 on the way count: a program that leaves them out, or rounds other values in their place, can miss the bound.
Values may be sent and summed in bfloat16 or wider, within the bound.
A program may use at most 64 MiB of HBM per device.

v0:
```python
import jax
import jax.numpy as jnp
from jax import lax
from jax.sharding import PartitionSpec as P

beta_first = 0.9
beta_second = 0.95
learn_rate = 0.001
adam_eps = 1e-08
adam_step = 100.0


def adam_update(gradient, master, first, second, used):
    first_new = beta_first * first + (1.0 - beta_first) * gradient
    second_new = beta_second * second + (1.0 - beta_second) * gradient * gradient
    corr_first = 1.0 - beta_first**adam_step
    corr_second = 1.0 - beta_second**adam_step
    master_new = master - learn_rate * (first_new / corr_first) / (
        jnp.sqrt(second_new / corr_second) + adam_eps
    )
    return (master_new * used, first_new * used, second_new * used)


def slot_targets(own_row, capacity):
    block_count = own_row.shape[0]
    order = jnp.arange(block_count, dtype=jnp.int32)
    earlier = (own_row[:, None] == own_row[None, :]) & (order[:, None] < order[None, :])
    return own_row * capacity + jnp.sum(earlier.astype(jnp.int32), axis=0)


def place_slots(gathered, target):
    every_slot = jnp.arange(gathered.shape[0], dtype=jnp.int32)
    placing = (target[:, None] == every_slot[None, :]).astype(jnp.bfloat16)
    placed = jnp.einsum("ks,srh->krh", placing, gathered, preferred_element_type=jnp.float32)
    return placed.astype(jnp.bfloat16).reshape(-1, gathered.shape[2])


def body(
    activation,
    w_query,
    key_rows,
    value_rows,
    out_grad,
    owners,
    master_copy,
    first_moment,
    second_moment,
):
    width_dp = lax.axis_size("dp")
    my_index = lax.axis_index("dp")
    capacity = master_copy.shape[0]
    block_rows = master_copy.shape[1]
    head_size = master_copy.shape[2]
    factor = head_size ** (-0.5)
    whole = lax.all_gather(activation, "tensor", axis=1, tiled=True)
    queries = jnp.dot(whole, w_query, preferred_element_type=jnp.float32).astype(jnp.bfloat16)
    scores = jnp.dot(queries, key_rows.T, preferred_element_type=jnp.float32) * factor
    length = scores.shape[0]
    row_pos = jnp.arange(length)[:, None]
    col_pos = jnp.arange(length)[None, :]
    scores = jnp.where(row_pos >= col_pos, scores, -1e30)
    shifted = jnp.exp(scores - jnp.max(scores, axis=1, keepdims=True))
    attention = shifted / jnp.sum(shifted, axis=1, keepdims=True)
    rounded = attention.astype(jnp.bfloat16)
    outputs = jnp.dot(rounded, value_rows, preferred_element_type=jnp.float32)
    deltas = jnp.sum(out_grad.astype(jnp.float32) * outputs, axis=1, keepdims=True)
    upstream = jnp.dot(out_grad, value_rows.T, preferred_element_type=jnp.float32)
    dscores = (attention * (upstream - deltas)).astype(jnp.bfloat16)
    dquery = (jnp.dot(dscores, key_rows, preferred_element_type=jnp.float32) * factor).astype(
        jnp.bfloat16
    )
    model_width = whole.shape[1]
    block_count = model_width // block_rows
    own_row = owners[0, :, 0]
    target = slot_targets(own_row, capacity)
    my_slots = my_index * capacity + jnp.arange(capacity, dtype=jnp.int32)
    pick = (target[None, :] == my_slots[:, None]).astype(jnp.float32)
    used = jnp.sum(pick, axis=1)[:, None, None]
    gradient = jnp.dot(whole.T, dquery, preferred_element_type=jnp.float32)
    blocks = gradient.reshape(block_count, block_rows, head_size)
    all_slots = jnp.arange(width_dp * capacity, dtype=jnp.int32)
    select = (target[None, :] == all_slots[:, None]).astype(jnp.float32)
    packed = jnp.einsum("sk,krh->srh", select, blocks, precision=lax.Precision.HIGHEST)
    packed = packed.reshape(width_dp, capacity * block_rows, head_size)
    arrived = lax.all_to_all(packed, "dp", split_axis=0, concat_axis=0, tiled=True)
    mine = jnp.sum(arrived, axis=0).reshape(capacity, block_rows, head_size)
    master_new, first_new, second_new = adam_update(
        mine, master_copy, first_moment, second_moment, used
    )
    gathered = lax.all_gather(master_new.astype(jnp.bfloat16), "dp", axis=0, tiled=True)
    weights_new = place_slots(gathered, target)
    return (weights_new, master_new, first_new, second_new)


def solution(mesh):
    return jax.shard_map(
        body,
        mesh=mesh,
        in_specs=(
            P("dp", "tensor"),
            P(None, "tensor"),
            P("dp", "tensor"),
            P("dp", "tensor"),
            P("dp", "tensor"),
            P("tensor", None, None),
            P("dp", None, "tensor"),
            P("dp", None, "tensor"),
            P("dp", None, "tensor"),
        ),
        out_specs=(
            P(None, "tensor"),
            P("dp", None, "tensor"),
            P("dp", None, "tensor"),
            P("dp", None, "tensor"),
        ),
        check_vma=False,
    )
```

profile of v0, /device:TPU:1, one launch (start us, length us, event | category | flops | bytes accessed | tf_op | source)
XLA Modules:
  0.0 764.3 jit_solution(15303378819685680809)
XLA Ops:
  7.2 0.0 all-gather.3.cloned.1.call-start
  7.2 0.7 all-gather.3.cloned.1.call-update
  7.9 1.0 copy.40
  9.0 0.8 convert_reduce_fusion
  9.8 0.7 multiply_add_fusion.1
  10.5 198.4 %all-gather.3.cloned.1.call-done = bf16[384,6656]{0,1:T(8,128)(2,1)} async-done(((bf16[384,832]{0,1:T(8,128)(2,1)}), bf16[384,6656]{0,1:T(8,128)(2,1)}) %all-gather.3.cloned.1.call-update) | async-done | bytes 5111824 | tf_op jit(solution)/shard_map/all_gather | solution.py:55
  208.8 4.3 fusion.30
  213.1 0.1 fusion.15
  213.2 0.3 fusion.13
  213.6 0.5 fusion.12
  214.1 6.0 convolution_bitcast_fusion
  220.0 5.0 copy.42
  225.0 7.6 fusion.2
  232.6 8.1 %copy.44 = f32[128,128,128]{2,1,0:T(8,128)} copy(f32[128,128,128]{2,0,1:T(8,128)S(1)} %fusion.2) | data formatting | bytes 16777216 | tf_op jit(solution)/shard_map/sk,krh->srh/dot_general | solution.py:83
  240.7 20.0 %all-to-all-start = ((f32[64,256,128]{2,1,0:T(8,128)}), f32[64,256,128]{2,1,0:T(8,128)}, u32[]{:S(2)}, u32[]{:S(2)}) async-start(f32[64,256,128]{2,1,0:T(8,128)} %bitcast.23), calls=%async_computation | async-start | bytes 16777216 | tf_op jit(solution)/shard_map/all_to_all | solution.py:85
  260.6 0.3 all-gather.5.cloned.1.call-start
  260.9 0.2 fusion.28
  261.1 365.3 %all-to-all-done = f32[64,256,128]{2,1,0:T(8,128)} async-done(((f32[64,256,128]{2,1,0:T(8,128)}), f32[64,256,128]{2,1,0:T(8,128)}, u32[]{:S(2)}, u32[]{:S(2)}) %all-to-all-start) | async-done | bytes 8388640 | tf_op jit(solution)/shard_map/all_to_all | solution.py:85
  626.4 3.8 reduce_sum.48
  630.2 0.9 fusion.29
  631.1 0.0 all-gather.5.cloned.1.call-update
  631.1 119.7 %all-gather.5.cloned.1.call-done = bf16[128,128,128]{2,1,0:T(8,128)(2,1)} async-done(((bf16[2,128,128]{2,1,0:T(8,128)(2,1)}), bf16[128,128,128]{2,1,0:T(8,128)(2,1)}) %all-gather.5.cloned.1.call-update) | async-done | bytes 4194320 | tf_op jit(solution)/shard_map/all_gather | solution.py:90
  750.8 5.0 fusion.4
  755.8 1.6 copy.46
  (15 shorter events, 0.0 us)
Async XLA Ops:
  7.2 201.7 %copy-start = (bf16[6656,128]{1,0:T(8,128)(2,1)S(1)}, bf16[6656,128]{1,0:T(8,128)(2,1)}, u32[]{:S(2)}) copy-start(bf16[6656,128]{1,0:T(8,128)(2,1)} %param.10) | copy-start | bytes 5111812
  7.2 201.6 %all-gather.3.cloned.1.call-start = ((), (), s32[]{:S(2)}) async-start(), calls=%async_computation.1 | async-start | bytes 5750784 | tf_op jit(solution)/shard_map/all_gather | solution.py:55
  7.9 205.3 %copy-start.6 = (bf16[384,128]{1,0:T(8,128)(2,1)S(1)}, bf16[384,128]{1,0:T(8,128)(2,1)}, u32[]{:S(2)}) copy-start(bf16[384,128]{1,0:T(8,128)(2,1)} %param.12) | copy-start | bytes 294916
  10.5 203.1 %copy-start.4 = (bf16[384,128]{1,0:T(8,128)(2,1)S(1)}, bf16[384,128]{1,0:T(8,128)(2,1)}, u32[]{:S(2)}) copy-start(bf16[384,128]{1,0:T(8,128)(2,1)} %param.13) | copy-start | bytes 294916
  10.5 203.1 %copy-start.5 = (bf16[384,128]{1,0:T(8,128)(2,1)S(1)}, bf16[384,128]{1,0:T(8,128)(2,1)}, u32[]{:S(2)}) copy-start(bf16[384,128]{1,0:T(8,128)(2,1)} %param.11) | copy-start | bytes 294916
  240.7 385.7 %all-to-all-start = ((f32[64,256,128]{2,1,0:T(8,128)}), f32[64,256,128]{2,1,0:T(8,128)}, u32[]{:S(2)}, u32[]{:S(2)}) async-start(f32[64,256,128]{2,1,0:T(8,128)} %bitcast.23), calls=%async_computation | async-start | bytes 16777216 | tf_op jit(solution)/shard_map/all_to_all | solution.py:85
  260.6 490.2 %all-gather.5.cloned.1.call-start = ((), (), s32[]{:S(2)}) async-start(), calls=%async_computation.2 | async-start | bytes 4259840 | tf_op jit(solution)/shard_map/all_gather | solution.py:90
  261.1 369.1 %copy-start.1 = (f32[2,128,128]{2,1,0:T(8,128)S(1)}, f32[2,128,128]{2,1,0:T(8,128)}, u32[]{:S(2)}) copy-start(f32[2,128,128]{2,1,0:T(8,128)} %param.15) | copy-start | bytes 393220
  261.1 369.1 %copy-start.2 = (f32[2,128,128]{2,1,0:T(8,128)S(1)}, f32[2,128,128]{2,1,0:T(8,128)}, u32[]{:S(2)}) copy-start(f32[2,128,128]{2,1,0:T(8,128)} %param.17) | copy-start | bytes 393220
  261.1 369.1 %copy-start.3 = (f32[2,128,128]{2,1,0:T(8,128)S(1)}, f32[2,128,128]{2,1,0:T(8,128)}, u32[]{:S(2)}) copy-start(f32[2,128,128]{2,1,0:T(8,128)} %param.16) | copy-start | bytes 393220
Sparse Core Ops, SparseCore 0:
  11.2 197.5 all-gather.2
  631.2 119.5 all-gather.4
where the time goes:
time: 765 us; the launch traced here: 764 us
  waiting for transfers between devices  684 us (89%)
  matrix products  23.7 us (3%)
  starting transfers between devices  20.3 us (3%)
  local copies, waits for them, and re-layouts  15.7 us (2%)
  between operations  14.2 us (2%)
    all_to_all x1, waiting for transfers between devices, body(): lax.all_to_all(packed, 'dp', split_axis=0, concat_axis=0, tiled=True)  365 us
    all_gather x1, waiting for transfers between devices, body(): whole = lax.all_gather(activation, 'tensor', axis=1, tiled=True)  198 us
    all_gather x1, waiting for transfers between devices, body(): lax.all_gather(master_new.astype(jnp.bfloat16), 'dp', axis=0, tiled=True)  120 us
    all_to_all x1, starting transfers between devices, body(): lax.all_to_all(packed, 'dp', split_axis=0, concat_axis=0, tiled=True)  20 us
  transfers between devices with their start and end apart: 3, of which 3 were waited for; matrix products, arithmetic and copies ran while one was open for 0% of the time, Pallas kernels for 0%

commit v1 on v0

v1 whole, which is shorter than its diff:
```python
import functools

import jax
import jax.numpy as jnp
from jax import lax
from jax.experimental import pallas as pl
from jax.experimental.pallas import tpu as pltpu
from jax.sharding import PartitionSpec as P

beta_first = 0.9
beta_second = 0.95
learn_rate = 0.001
adam_eps = 1e-08
adam_step = 100.0

MESH = pl.DeviceIdType.MESH
TOK = 384
FEAT = 832
HD = 128
NBLK = 52
HALF = 26
SUB = 16
UNITS = 13
CHUNKS = 3
CTOK = TOK // CHUNKS


def adam_update(gradient, master, first, second, used):
    first_new = beta_first * first + (1.0 - beta_first) * gradient
    second_new = beta_second * second + (1.0 - beta_second) * gradient * gradient
    corr_first = 1.0 - beta_first**adam_step
    corr_second = 1.0 - beta_second**adam_step
    master_new = master - learn_rate * (first_new / corr_first) / (
        jnp.sqrt(second_new / corr_second) + adam_eps
    )
    return (master_new * used, first_new * used, second_new * used)


def dot_t(a, b):
    return lax.dot_general(a, b, (((1,), (1,)), ((), ())), preferred_element_type=jnp.float32)


def dot_0(a, b):
    return lax.dot_general(a, b, (((0,), (0,)), ((), ())), preferred_element_type=jnp.float32)


def kernel(
    block_of, used_of, slot_of,
    act, w, keys, values, outg, master, first, second,
    out_w, out_m, out_f, out_s,
    whole, sib, qacc, dq, grad, recv_y, gsum, recv_z, gall, send_g, recv_g, send_w, recv_w, wall,
    z_s, z_r, x_s, x_r, f_s, f_r, s_s, s_r, d_s, d_r, y_s, y_r, r_s, r_r, a_s, a_r,
    o_s, o_r, b_s, b_r, w_s, w_r, v_s, v_r, c_s, c_r, l_sem,
):
    dp = lax.axis_index("dp")
    t = lax.axis_index("tensor")
    zl = dp // 8
    part = lax.rem(dp, 8)
    y = part // 2
    c = lax.rem(part, 2)
    a = t // 4
    x = lax.rem(t, 4)

    def at_x(d):
        return (dp, a * 4 + lax.rem(x + d, 4))

    opposite = (dp, (1 - a) * 4 + x)
    sibling = (zl * 8 + y * 2 + (1 - c), t)

    def at_part(p):
        return (zl * 8 + p, t)

    def at_z(z):
        return (z * 8 + part, t)

    barrier = pltpu.get_barrier_semaphore()
    peers = [at_x(d) for d in (1, 2, 3)] + [opposite]
    peers += [at_part(lax.rem(part + d, 8)) for d in range(1, 8)]
    peers += [at_z(lax.rem(zl + d, 8)) for d in range(1, 8)]
    for peer in peers:
        pl.semaphore_signal(barrier, inc=1, device_id=peer, device_id_type=MESH)
    pl.semaphore_wait(barrier, len(peers))

    def remote(src, dst, ss, rs, dev):
        return pltpu.make_async_remote_copy(
            src_ref=src, dst_ref=dst, send_sem=ss, recv_sem=rs, device_id=dev, device_id_type=MESH
        )

    own = pltpu.make_async_copy(act, whole.at[t], l_sem)
    own.start()
    rows = [pl.ds(i * CTOK, CTOK) for i in range(CHUNKS)]
    cross = [
        remote(act.at[r], whole.at[t, r], z_s.at[i], z_r.at[i], opposite) for i, r in enumerate(rows)
    ]
    for cp in cross:
        cp.start()
    along = []
    for i, r in enumerate(rows):
        for d in (1, 3, 2):
            cp = remote(act.at[r], whole.at[t, r], x_s.at[d - 1, i], x_r.at[d - 1, i], at_x(d))
            cp.start()
            along.append(cp)
    t_op = (1 - a) * 4 + x
    onward = []
    for i, r in enumerate(rows):
        cross[i].wait_recv()
        for d in (1, 3, 2):
            cp = remote(whole.at[t_op, r], whole.at[t_op, r], f_s.at[d - 1, i], f_r.at[d - 1, i], at_x(d))
            cp.start()
            onward.append(cp)
    own.wait()
    for cp in along:
        cp.wait_recv()
    for cp in onward:
        cp.wait_recv()
    share = []
    for j in range(4):
        cp = remote(whole.at[(1 - c) * 4 + j], sib.at[j], s_s.at[j], s_r.at[j], sibling)
        cp.start()
        share.append(cp)

    qacc[...] = jnp.zeros_like(qacc)

    def add_q(k, carry):
        qacc[...] += jnp.dot(whole[k], w[k], preferred_element_type=jnp.float32)
        return carry

    lax.fori_loop(0, 8, add_q, 0)
    factor = HD ** (-0.5)
    for i in range(CHUNKS):
        n = (i + 1) * CTOK
        r = rows[i]
        kk = keys[pl.ds(0, n)]
        vv = values[pl.ds(0, n)]
        og = outg[r]
        scores = dot_t(qacc[r].astype(jnp.bfloat16), kk) * factor
        row_pos = lax.broadcasted_iota(jnp.int32, (CTOK, n), 0) + i * CTOK
        col_pos = lax.broadcasted_iota(jnp.int32, (CTOK, n), 1)
        scores = jnp.where(row_pos >= col_pos, scores, -1e30)
        shifted = jnp.exp(scores - jnp.max(scores, axis=1, keepdims=True))
        attention = shifted / jnp.sum(shifted, axis=1, keepdims=True)
        outputs = jnp.dot(attention.astype(jnp.bfloat16), vv, preferred_element_type=jnp.float32)
        deltas = jnp.sum(og.astype(jnp.float32) * outputs, axis=1, keepdims=True)
        upstream = dot_t(og, vv)
        dscores = (attention * (upstream - deltas)).astype(jnp.bfloat16)
        dquery = jnp.dot(dscores, kk, preferred_element_type=jnp.float32) * factor
        dq[0, r] = dquery.astype(jnp.bfloat16)
    swap = remote(dq.at[0], dq.at[1], d_s, d_r, sibling)
    swap.start()
    swap.wait_recv()
    for cp in share:
        cp.wait_recv()
    for j in range(4):
        g = dot_0(whole[c * 4 + j], dq[0]) + dot_0(sib[j], dq[1])
        for m in range(13):
            k = j * 13 + m
            grad[k // 2, k % 2] = g[m * 64 : (m + 1) * 64]

    to_parts = []
    for d in range(1, 8):
        p = lax.rem(part + d, 8)
        src = grad.at[:, p // 4, pl.ds(pl.multiple_of(lax.rem(p, 4) * SUB, SUB), SUB)]
        cp = remote(src, recv_y.at[part], y_s.at[d - 1], y_r.at[d - 1], at_part(p))
        cp.start()
        to_parts.append(cp)
    recv_y[part] = grad[:, part // 4, pl.ds(pl.multiple_of(lax.rem(part, 4) * SUB, SUB), SUB)]
    for cp in to_parts:
        cp.wait_recv()

    def add_y(k, carry):
        for h in range(2):
            total = recv_y[h, k] + recv_y[2 + h, k] + recv_y[4 + h, k] + recv_y[6 + h, k]
            gsum[pl.ds((h * HALF + k) * 2, 2)] = total.reshape(2, 8, HD)
        return carry

    lax.fori_loop(0, HALF, add_y, 0)

    def piece(z):
        return pl.ds(z * UNITS, UNITS)

    to_z = []
    for d in range(1, 8):
        z = lax.rem(zl + d, 8)
        cp = remote(gsum.at[piece(z)], recv_z.at[zl], r_s.at[d - 1], r_r.at[d - 1], at_z(z))
        cp.start()
        to_z.append(cp)
    recv_z[zl] = gsum[piece(zl)]
    for cp in to_z:
        cp.wait_recv()
    total = recv_z[0]
    for z in range(1, 8):
        total = total + recv_z[z]
    gall[piece(zl)] = total
    back_z = []
    for d in range(1, 8):
        z = lax.rem(zl + d, 8)
        cp = remote(gall.at[piece(zl)], gall.at[piece(zl)], a_s.at[d - 1], a_r.at[d - 1], at_z(z))
        cp.start()
        back_z.append(cp)
    for cp in back_z:
        cp.wait_recv()

    for p in range(8):
        for j in range(2):
            k = block_of[zl * 16 + p * 2 + j]
            send_g[p, j, 0:8] = gall[k * 2]
            send_g[p, j, 8:16] = gall[k * 2 + 1]
    to_owner = []
    for d in range(1, 8):
        p = lax.rem(part + d, 8)
        cp = remote(send_g.at[p], recv_g.at[part], o_s.at[d - 1], o_r.at[d - 1], at_part(p))
        cp.start()
        to_owner.append(cp)
    recv_g[part] = send_g[part]
    for cp in to_owner:
        cp.wait_recv()
    for j in range(2):
        used = used_of[dp * 2 + j]
        for p in range(8):
            r = pl.ds(p * SUB, SUB)
            nm, nf, ns = adam_update(recv_g[p, j], master[j, r], first[j, r], second[j, r], used)
            out_m[j, r] = nm
            out_f[j, r] = nf
            out_s[j, r] = ns
            send_w[p, j] = nm.astype(jnp.bfloat16)

    to_rows = []
    for d in range(1, 8):
        p = lax.rem(part + d, 8)
        cp = remote(send_w.at[p], recv_w.at[pl.ds(part * 2, 2)], b_s.at[d - 1], b_r.at[d - 1], at_part(p))
        cp.start()
        to_rows.append(cp)
    recv_w[pl.ds(part * 2, 2)] = send_w[part]
    for cp in to_rows:
        cp.wait_recv()
    wall[pl.ds(zl * 16, 16)] = recv_w[...]
    all_z = []
    for d in range(1, 8):
        z = lax.rem(zl + d, 8)
        cp = remote(recv_w, wall.at[pl.ds(zl * 16, 16)], w_s.at[d - 1], w_r.at[d - 1], at_z(z))
        cp.start()
        all_z.append(cp)
    for cp in all_z:
        cp.wait_recv()
    mine = pl.ds(pl.multiple_of(part * SUB, SUB), SUB)

    def place(k, carry):
        out_w[k, mine] = wall[slot_of[k]]
        return carry

    lax.fori_loop(0, NBLK, place, 0)
    to_y = []
    for d in (1, 3, 2):
        p = lax.rem(y + d, 4) * 2 + c
        cp = remote(out_w.at[:, mine], out_w.at[:, mine], v_s.at[d - 1], v_r.at[d - 1], at_part(p))
        cp.start()
        to_y.append(cp)
    to_core = [remote(out_w.at[:, mine], out_w.at[:, mine], c_s.at[0], c_r.at[0], sibling)]
    to_core[0].start()
    for n, d in enumerate((1, 3, 2)):
        to_y[n].wait_recv()
        p = lax.rem(y - d + 4, 4) * 2 + c
        r = pl.ds(pl.multiple_of(p * SUB, SUB), SUB)
        cp = remote(out_w.at[:, r], out_w.at[:, r], c_s.at[d], c_r.at[d], sibling)
        cp.start()
        to_core.append(cp)
    for cp in to_core:
        cp.wait_recv()
    sent = cross + along + onward + share + [swap] + to_parts + to_z + back_z
    for cp in sent + to_owner + to_rows + all_z + to_y + to_core:
        cp.wait_send()


def body(
    activation, w_query, key_rows, value_rows, out_grad, owners, master_copy, first_moment, second_moment
):
    own_row = owners[0, :, 0]
    order = jnp.arange(NBLK, dtype=jnp.int32)
    earlier = (own_row[:, None] == own_row[None, :]) & (order[:, None] < order[None, :])
    target = own_row * 2 + jnp.sum(earlier.astype(jnp.int32), axis=0)
    match = target[None, :] == jnp.arange(128, dtype=jnp.int32)[:, None]
    block_of = jnp.sum(jnp.where(match, order[None, :], 0), axis=1)
    used_of = jnp.sum(match.astype(jnp.float32), axis=1)
    smem = pl.BlockSpec(memory_space=pltpu.SMEM)
    vmem = pl.BlockSpec(memory_space=pltpu.VMEM)
    f32 = jnp.float32
    bf16 = jnp.bfloat16
    dma = pltpu.SemaphoreType.DMA
    new_w, new_m, new_f, new_s = pl.pallas_call(
        kernel,
        out_shape=(
            jax.ShapeDtypeStruct((NBLK, 128, HD), bf16),
            jax.ShapeDtypeStruct((2, 128, HD), f32),
            jax.ShapeDtypeStruct((2, 128, HD), f32),
            jax.ShapeDtypeStruct((2, 128, HD), f32),
        ),
        in_specs=[smem] * 3 + [vmem] * 8,
        out_specs=(vmem,) * 4,
        scratch_shapes=[
            pltpu.VMEM((8, TOK, FEAT), bf16),
            pltpu.VMEM((4, TOK, FEAT), bf16),
            pltpu.VMEM((TOK, HD), f32),
            pltpu.VMEM((2, TOK, HD), bf16),
            pltpu.VMEM((HALF, 2, 64, HD), f32),
            pltpu.VMEM((8, HALF, SUB, HD), f32),
            pltpu.VMEM((8 * UNITS, 8, HD), f32),
            pltpu.VMEM((8, UNITS, 8, HD), f32),
            pltpu.VMEM((8 * UNITS, 8, HD), f32),
            pltpu.VMEM((8, 2, SUB, HD), f32),
            pltpu.VMEM((8, 2, SUB, HD), f32),
            pltpu.VMEM((8, 2, SUB, HD), bf16),
            pltpu.VMEM((16, SUB, HD), bf16),
            pltpu.VMEM((128, SUB, HD), bf16),
            dma((CHUNKS,)), dma((CHUNKS,)),
            dma((3, CHUNKS)), dma((3, CHUNKS)),
            dma((3, CHUNKS)), dma((3, CHUNKS)),
            dma((4,)), dma((4,)),
            dma, dma,
            dma((7,)), dma((7,)),
            dma((7,)), dma((7,)),
            dma((7,)), dma((7,)),
            dma((7,)), dma((7,)),
            dma((7,)), dma((7,)),
            dma((7,)), dma((7,)),
            dma((3,)), dma((3,)),
            dma((4,)), dma((4,)),
            dma,
        ],
        compiler_params=pltpu.CompilerParams(
            collective_id=0, has_side_effects=True, vmem_limit_bytes=56 * 2**20
        ),
        name="project_back",
    )(
        block_of, used_of, target,
        activation, w_query.reshape(8, FEAT, HD), key_rows, value_rows, out_grad,
        master_copy, first_moment, second_moment,
    )
    return (new_w.reshape(NBLK * 128, HD), new_m, new_f, new_s)


def solution(mesh):
    return jax.shard_map(
        body,
        mesh=mesh,
        in_specs=(
            P("dp", "tensor"),
            P(None, "tensor"),
            P("dp", "tensor"),
            P("dp", "tensor"),
            P("dp", "tensor"),
            P("tensor", None, None),
            P("dp", None, "tensor"),
            P("dp", None, "tensor"),
            P("dp", None, "tensor"),
        ),
        out_specs=(
            P(None, "tensor"),
            P("dp", None, "tensor"),
            P("dp", None, "tensor"),
            P("dp", None, "tensor"),
        ),
        check_vma=False,
    )
```

time: 765 us -> 215 us (0.28)
  the two profiles are of different devices: /device:TPU:1 before, /device:TPU:97 now
where the time goes in v1:
time: 215 us; the launch traced here: 214 us
  Pallas kernels  204 us (95%)
  local copies, waits for them, and re-layouts  6.98 us (3%)
  other arithmetic  2.68 us (1%)
    pallas_call x1, Pallas kernels, body(): pl.pallas_call(kernel, out_shape=(jax.ShapeDtypeStruct((NBLK, 128, HD), b...  204 us
    unnamed x13, local copies, waits for them, and re-layouts  6.98 us

profile of v1, /device:TPU:97, one launch (start us, length us, event | category | flops | bytes accessed | tf_op | source)
XLA Modules:
  0.0 214.4 jit_solution(17834951359700727471)
XLA Ops:
  0.6 0.8 convert_reduce_fusion.1
  1.5 0.7 multiply_add_fusion.slot_of
  2.1 0.0 copy-start.3
  2.1 0.6 convert_reduce_fusion.used_of
  2.7 0.6 select_reduce_fusion.block_of
  3.3 2.2 %copy.14.act = bf16[384,832]{1,0:T(8,128)(2,1)} copy(bf16[384,832]{0,1:T(8,128)(2,1)} %param.9) | data formatting | bytes 1277952 | tf_op args[0]
  5.5 0.0 copy-done.3
  5.5 204.1 %project_back.1 = (bf16[52,128,128]{2,1,0:T(8,128)(2,1)}, f32[2,128,128]{2,1,0:T(8,128)}, f32[2,128,128]{2,1,0:T(8,128)}, f32[2,128,128]{2,1,0:T(8,128)}) custom-call(s32[128]{0:T(128)} %select_reduce_fusion.block_of, f32[128]{0:T(128)} %convert_reduce_fusion.used_of, s32[52]{0:T(128)} %copy-done.3, bf16[384,832]{1,0:T(8,128)(2,1)} %copy.14.act, ...), custom_call_target="tpu_custom_call" | custom-call | tf_op jit(solution)/shard_map/project_back/pallas_call | solution.py:289
  209.6 0.0 copy-start.2
  209.6 0.0 copy-start.1
  209.6 0.0 copy-start
  209.6 2.8 %copy.19 = bf16[6656,128]{1,0:T(8,128)(2,1)} copy(bf16[6656,128]{1,0:T(8,128)(2,1)} %bitcast.5) | data formatting | bytes 3407872
  212.4 0.0 copy-done.2
  212.4 0.7 copy.20
  213.1 0.0 copy-done.1
  213.1 0.7 copy.21
  213.7 0.0 copy-done
  213.7 0.7 copy.22
Async XLA Ops:
  2.1 3.4 %copy-start.3 = (s32[52]{0:T(128)}, s32[52]{0:T(128)S(1)}, u32[]{:S(2)}) copy-start(s32[52]{0:T(128)S(1)} %multiply_add_fusion.slot_of) | copy-start | bytes 628
  209.6 2.8 %copy-start.2 = (f32[2,128,128]{2,1,0:T(8,128)S(1)}, f32[2,128,128]{2,1,0:T(8,128)}, u32[]{:S(2)}) copy-start(f32[2,128,128]{2,1,0:T(8,128)} %get-tuple-element.17) | copy-start | bytes 393220
  209.6 3.5 %copy-start.1 = (f32[2,128,128]{2,1,0:T(8,128)S(1)}, f32[2,128,128]{2,1,0:T(8,128)}, u32[]{:S(2)}) copy-start(f32[2,128,128]{2,1,0:T(8,128)} %get-tuple-element.18) | copy-start | bytes 393220
  209.6 4.1 %copy-start = (f32[2,128,128]{2,1,0:T(8,128)S(1)}, f32[2,128,128]{2,1,0:T(8,128)}, u32[]{:S(2)}) copy-start(f32[2,128,128]{2,1,0:T(8,128)} %get-tuple-element.19) | copy-start | bytes 393220

commit v2 on v1

v2 whole, which is shorter than its diff:
```python
import functools

import jax
import jax.numpy as jnp
from jax import lax
from jax.experimental import pallas as pl
from jax.experimental.pallas import tpu as pltpu
from jax.sharding import PartitionSpec as P

beta_first = 0.9
beta_second = 0.95
learn_rate = 0.001
adam_eps = 1e-08
adam_step = 100.0

MESH = pl.DeviceIdType.MESH
TOK = 384
FEAT = 832
HD = 128
NBLK = 52
HALF = 26
HROWS = HALF * 128
SUB = 16
OWN = 7
PAD = 8 * OWN
CHUNKS = 3
CTOK = TOK // CHUNKS
LEVELS = 32700.0
FIXED = 32766.0
TOP_MASTER = 0.078125
TOP_FIRST = 4.0
TOP_SECOND = 1.0


def adam_update(gradient, master, first, second, used):
    first_new = beta_first * first + (1.0 - beta_first) * gradient
    second_new = beta_second * second + (1.0 - beta_second) * gradient * gradient
    corr_first = 1.0 - beta_first**adam_step
    corr_second = 1.0 - beta_second**adam_step
    master_new = master - learn_rate * (first_new / corr_first) / (
        jnp.sqrt(second_new / corr_second) + adam_eps
    )
    return (master_new * used, first_new * used, second_new * used)


def dot_t(a, b):
    return lax.dot_general(a, b, (((1,), (1,)), ((), ())), preferred_element_type=jnp.float32)


def dot_0(a, b):
    return lax.dot_general(a, b, (((0,), (0,)), ((), ())), preferred_element_type=jnp.float32)


def pack(v, inv):
    q = jnp.round(v * inv).astype(jnp.int32)
    return (q[:8] << 16) | (q[8:] & 0xFFFF)


def unpack(u, step):
    return jnp.concatenate([u >> 16, (u << 16) >> 16], axis=0).astype(jnp.float32) * step


def level(top):
    bits = jnp.log(jnp.maximum(top, 1e-30)) * (8.0 / 0.6931471805599453)
    return jnp.ceil(bits).astype(jnp.int32)


def step_of(e):
    return jnp.exp(e.astype(jnp.float32) * (0.6931471805599453 / 8.0)) * (1.0 / LEVELS)


def inverse_of(e):
    return jnp.exp(e.astype(jnp.float32) * (-0.6931471805599453 / 8.0)) * LEVELS


def kernel(
    slot_code, block_code,
    act, w, keys, values, outg, master, first, second,
    out_w, out_m, out_f, out_s,
    whole, sib, wt, dq, grad, ys, yr, gsum, zs, zr, red, gq, sys, syr, szs, szr, send_g, recv_g,
    z_s, z_r, x_s, x_r, f_s, f_r, s_s, s_r, d_s, d_r, y_s, y_r, r_s, r_r, a_s, a_r,
    o_s, o_r, w_s, w_r, v_s, v_r, c_s, c_r, k_s, k_r, p_s, p_r, l_sem,
):
    dp = lax.axis_index("dp")
    t = lax.axis_index("tensor")
    zl = dp // 8
    part = lax.rem(dp, 8)
    y = part // 2
    c = lax.rem(part, 2)
    a = t // 4
    x = lax.rem(t, 4)
    f32 = jnp.float32

    def at_x(d):
        return (dp, a * 4 + lax.rem(x + d, 4))

    opposite = (dp, (1 - a) * 4 + x)
    sibling = (zl * 8 + y * 2 + (1 - c), t)

    def at_part(p):
        return (zl * 8 + p, t)

    def at_z(z):
        return (z * 8 + part, t)

    barrier = pltpu.get_barrier_semaphore()
    peers = [at_x(d) for d in (1, 2, 3)] + [opposite]
    peers += [at_part(lax.rem(part + d, 8)) for d in range(1, 8)]
    peers += [at_z(lax.rem(zl + d, 8)) for d in range(1, 8)]
    for peer in peers:
        pl.semaphore_signal(barrier, inc=1, device_id=peer, device_id_type=MESH)
    pl.semaphore_wait(barrier, len(peers))
    sent = []

    def go(src, dst, ss, rs, dev):
        cp = pltpu.make_async_remote_copy(
            src_ref=src, dst_ref=dst, send_sem=ss, recv_sem=rs, device_id=dev, device_id_type=MESH
        )
        cp.start()
        sent.append(cp)
        return cp

    def rows(start, n, unit):
        return pl.ds(pl.multiple_of(start, unit), n)

    cols = [pl.ds(i * CTOK, CTOK) for i in range(CHUNKS)]
    mine = rows(t * FEAT, FEAT, 16)
    own = pltpu.make_async_copy(act, whole.at[mine], l_sem)
    own.start()
    cross = []
    for i in range(CHUNKS):
        for s in range(2):
            cross.append(
                go(
                    act.at[pl.ds(s * 416, 416), cols[i]],
                    whole.at[rows(t * FEAT + s * 416, 416, 16), cols[i]],
                    z_s.at[i, s], z_r.at[i, s], opposite,
                )
            )
    along = [
        [
            go(act.at[:, cols[i]], whole.at[mine, cols[i]], x_s.at[d - 1, i], x_r.at[d - 1, i], at_x(d))
            for d in (1, 3, 2)
        ]
        for i in range(CHUNKS)
    ]
    onward = [[], [], []]

    def pass_on(n):
        i, s = n // 2, n % 2
        cross[n].wait_recv()
        r = rows(((1 - a) * 4 + x) * FEAT + s * 416, 416, 16)
        for d in (1, 3, 2):
            onward[i].append(
                go(
                    whole.at[r, cols[i]], whole.at[r, cols[i]],
                    f_s.at[d - 1, i, s], f_r.at[d - 1, i, s], at_x(d),
                )
            )

    def states(p, carry):
        r = rows(p * SUB, SUB, SUB)
        for j in range(2):
            sys[p, j] = pack(master[j, r], FIXED / TOP_MASTER)
            sys[p, 2 + j] = pack(first[j, r], FIXED / TOP_FIRST)
            sys[p, 4 + j] = pack(second[j, r], FIXED / TOP_SECOND)
        return carry

    lax.fori_loop(0, 8, states, 0)
    state_y = []
    for d in range(1, 8):
        p = lax.rem(part + d, 8)
        state_y.append(
            go(sys.at[p], syr.at[pl.ds(part * 6, 6)], k_s.at[d - 1], k_r.at[d - 1], at_part(p))
        )
    syr[pl.ds(part * 6, 6)] = sys[part]

    def turn(k, carry):
        wt[k] = w[k].astype(f32).T.astype(jnp.bfloat16)
        return carry

    lax.fori_loop(0, NBLK, turn, 0)
    grad[...] = jnp.zeros_like(grad)
    share = []
    swap = []
    factor = HD ** (-0.5)
    half = rows(c * HROWS, HROWS, 16)
    other = rows((1 - c) * HROWS, HROWS, 16)

    def attend(i):
        if i == 0:
            own.wait()
        for cp in along[i] + onward[i]:
            cp.wait_recv()
        share.append(
            go(whole.at[other, cols[i]], sib.at[:, cols[i]], s_s.at[i], s_r.at[i], sibling)
        )

        def add_q(k, total):
            for m in range(4):
                r = rows((k * 4 + m) * 128, 128, 128)
                total = total + jnp.dot(wt[k * 4 + m], whole[r, cols[i]], preferred_element_type=f32)
            return total

        qt = lax.fori_loop(0, 13, add_q, jnp.zeros((HD, CTOK), f32))
        queries = qt.T.astype(jnp.bfloat16)
        n = (i + 1) * CTOK
        kk = keys[pl.ds(0, n)]
        vv = values[pl.ds(0, n)]
        og = outg[cols[i]]
        scores = dot_t(queries, kk) * factor
        row_pos = lax.broadcasted_iota(jnp.int32, (CTOK, n), 0) + i * CTOK
        col_pos = lax.broadcasted_iota(jnp.int32, (CTOK, n), 1)
        scores = jnp.where(row_pos >= col_pos, scores, -1e30)
        shifted = jnp.exp(scores - jnp.max(scores, axis=1, keepdims=True))
        attention = shifted / jnp.sum(shifted, axis=1, keepdims=True)
        outputs = jnp.dot(attention.astype(jnp.bfloat16), vv, preferred_element_type=f32)
        deltas = jnp.sum(og.astype(f32) * outputs, axis=1, keepdims=True)
        upstream = dot_t(og, vv)
        dscores = (attention * (upstream - deltas)).astype(jnp.bfloat16)
        dquery = jnp.dot(dscores, kk, preferred_element_type=f32) * factor
        dq[0, cols[i]] = dquery.astype(jnp.bfloat16)
        swap.append(go(dq.at[0, cols[i]], dq.at[1, cols[i]], d_s.at[i], d_r.at[i], sibling))

    def add_grad(lo, n):
        tok = pl.ds(lo, n)

        def one(j, top):
            r = rows(j * FEAT, FEAT, 16)
            g = grad[r] + jnp.dot(whole[rows(c * HROWS + j * FEAT, FEAT, 16), tok], dq[0, tok], preferred_element_type=f32)
            g = g + jnp.dot(sib[r, tok], dq[1, tok], preferred_element_type=f32)
            grad[r] = g
            return jnp.maximum(top, jnp.max(jnp.abs(g), axis=0, keepdims=True))

        return lax.fori_loop(0, 4, one, jnp.zeros((1, HD), f32))

    pass_on(0)
    pass_on(1)
    pass_on(2)
    pass_on(3)
    attend(0)
    pass_on(4)
    attend(1)
    pass_on(5)

    for cp in state_y:
        cp.wait_recv()

    def states_z(z, carry):
        for j in range(OWN):
            u = block_code[z * OWN + j] & 63
            for m in range(3):
                szs[z, m * OWN + j] = syr[u + 2 * m]
        return carry

    lax.fori_loop(0, 8, states_z, 0)
    state_z = []
    for d in range(1, 8):
        z = lax.rem(zl + d, 8)
        state_z.append(
            go(szs.at[z], szr.at[pl.ds(zl * 3 * OWN, 3 * OWN)], p_s.at[d - 1], p_r.at[d - 1], at_z(z))
        )
    szr[pl.ds(zl * 3 * OWN, 3 * OWN)] = szs[zl]
    for i in range(2):
        share[i].wait_recv()
        swap[i].wait_recv()
    add_grad(0, 2 * CTOK)
    attend(2)
    share[2].wait_recv()
    swap[2].wait_recv()
    top = add_grad(2 * CTOK, CTOK)

    e = jnp.broadcast_to(level(top), (8, HD))
    inv = inverse_of(e[:1])

    def to_fixed(b, carry):
        for p in range(8):
            ys[p, b] = pack(grad[rows(b * 128 + p * SUB, SUB, SUB)], inv)
        return carry

    lax.fori_loop(0, HALF, to_fixed, 0)
    for p in range(8):
        ys[p, HALF] = e
    to_parts = []
    for d in range(1, 8):
        p = lax.rem(part + d, 8)
        to_parts.append(go(ys.at[p], yr.at[part], y_s.at[d - 1], y_r.at[d - 1], at_part(p)))
    yr[part] = ys[part]
    for cp in to_parts:
        cp.wait_recv()
    steps = [step_of(yr[p, HALF, 0:1]) for p in range(8)]

    def add_y(b, top):
        for h in range(2):
            total = unpack(yr[h, b], steps[h])
            for m in range(1, 4):
                total = total + unpack(yr[2 * m + h, b], steps[2 * m + h])
            gsum[h * HALF + b] = total
            top = jnp.maximum(top, jnp.max(jnp.abs(total), axis=0, keepdims=True))
        return top

    top = lax.fori_loop(0, HALF, add_y, jnp.zeros((1, HD), f32))
    gsum[pl.ds(NBLK, PAD - NBLK)] = jnp.zeros((PAD - NBLK, SUB, HD), f32)

    e = jnp.broadcast_to(level(top), (8, HD))
    inv = inverse_of(e[:1])

    def to_fixed_z(z, carry):
        for j in range(OWN):
            zs[z, j] = pack(gsum[z * OWN + j], inv)
        zs[z, OWN] = e
        return carry

    lax.fori_loop(0, 8, to_fixed_z, 0)
    to_z = []
    for d in range(1, 8):
        z = lax.rem(zl + d, 8)
        to_z.append(go(zs.at[z], zr.at[zl], r_s.at[d - 1], r_r.at[d - 1], at_z(z)))
    zr[zl] = zs[zl]
    for cp in to_z + state_z:
        cp.wait_recv()
    steps = [step_of(zr[z, OWN, 0:1]) for z in range(8)]
    top = jnp.zeros((1, HD), f32)
    part_rows = rows(part * SUB, SUB, SUB)
    for j in range(OWN):
        total = unpack(zr[0, j], steps[0])
        for z in range(1, 8):
            total = total + unpack(zr[z, j], steps[z])
        red[j] = total
        top = jnp.maximum(top, jnp.max(jnp.abs(total), axis=0, keepdims=True))
        u = block_code[zl * OWN + j] >> 6
        m_state = unpack(szr[u + j], TOP_MASTER / FIXED)
        f_state = unpack(szr[u + OWN + j], TOP_FIRST / FIXED)
        s_state = unpack(szr[u + 2 * OWN + j], TOP_SECOND / FIXED)
        nm, _, _ = adam_update(total, m_state, f_state, s_state, 1.0)
        out_w[zl * OWN + j, part_rows] = nm.astype(jnp.bfloat16)

    def weights(z, r):
        return out_w.at[pl.ds(z * OWN, OWN), r]

    w_z = []
    for d in range(1, 8):
        z = lax.rem(zl + d, 8)
        w_z.append(go(weights(zl, part_rows), weights(zl, part_rows), w_s.at[d - 1], w_r.at[d - 1], at_z(z)))
    e = jnp.broadcast_to(level(top), (8, HD))
    inv = inverse_of(e[:1])
    for j in range(OWN):
        gq[zl * 8 + j] = pack(red[j], inv)
    gq[zl * 8 + OWN] = e
    g_z = []
    for d in range(1, 8):
        z = lax.rem(zl + d, 8)
        at = gq.at[pl.ds(zl * 8, 8)]
        g_z.append(go(at, at, a_s.at[d - 1], a_r.at[d - 1], at_z(z)))

    to_y = []
    to_core = []
    for d in range(8):
        z = lax.rem(zl - d + 8, 8)
        if d:
            w_z[d - 1].wait_recv()
        at = weights(z, part_rows)
        to_y.append(
            [
                go(at, at, v_s.at[q - 1, d], v_r.at[q - 1, d], at_part(lax.rem(y + q, 4) * 2 + c))
                for q in (1, 3, 2)
            ]
        )
        to_core.append(go(at, at, c_s.at[0, d], c_r.at[0, d], sibling))

    for cp in g_z:
        cp.wait_recv()
    for p in range(8):
        for j in range(2):
            u = slot_code[zl * 16 + p * 2 + j] & 63
            send_g[p, j] = unpack(gq[u], step_of(gq[u | OWN][:1]))
    to_owner = []
    for d in range(1, 8):
        p = lax.rem(part + d, 8)
        to_owner.append(go(send_g.at[p], recv_g.at[part], o_s.at[d - 1], o_r.at[d - 1], at_part(p)))
    recv_g[part] = send_g[part]
    for d in range(8):
        z = lax.rem(zl - d + 8, 8)
        for n, q in enumerate((1, 3, 2)):
            to_y[d][n].wait_recv()
            r = rows((lax.rem(y - q + 4, 4) * 2 + c) * SUB, SUB, SUB)
            at = weights(z, r)
            to_core.append(go(at, at, c_s.at[q, d], c_r.at[q, d], sibling))
    for cp in to_owner:
        cp.wait_recv()
    for j in range(2):
        used = (slot_code[dp * 2 + j] >> 6).astype(f32)
        for p in range(8):
            r = pl.ds(p * SUB, SUB)
            nm, nf, ns = adam_update(recv_g[p, j], master[j, r], first[j, r], second[j, r], used)
            out_m[j, r] = nm
            out_f[j, r] = nf
            out_s[j, r] = ns
    for cp in to_core:
        cp.wait_recv()
    for cp in sent:
        cp.wait_send()


def body(
    activation, w_query, key_rows, value_rows, out_grad, owners, master_copy, first_moment, second_moment
):
    own_row = owners[0, :, 0]
    order = jnp.arange(NBLK, dtype=jnp.int32)
    earlier = (own_row[:, None] == own_row[None, :]) & (order[:, None] < order[None, :])
    second_slot = jnp.sum(earlier.astype(jnp.int32), axis=0)
    target = own_row * 2 + second_slot
    match = target[None, :] == jnp.arange(128, dtype=jnp.int32)[:, None]
    place = 64 + (order // OWN) * 8 + order % OWN
    slot_code = jnp.sum(jnp.where(match, place[None, :], 0), axis=1)
    block_code = (own_row // 8) * (3 * OWN * 64) + (own_row % 8) * 6 + second_slot
    block_code = jnp.pad(block_code, (0, PAD - NBLK))
    smem = pl.BlockSpec(memory_space=pltpu.SMEM)
    vmem = pl.BlockSpec(memory_space=pltpu.VMEM)
    f32 = jnp.float32
    bf16 = jnp.bfloat16
    i32 = jnp.int32
    dma = pltpu.SemaphoreType.DMA

    def pair(*dims):
        return [dma(dims), dma(dims)]

    new_w, new_m, new_f, new_s = pl.pallas_call(
        kernel,
        out_shape=(
            jax.ShapeDtypeStruct((PAD, 128, HD), bf16),
            jax.ShapeDtypeStruct((2, 128, HD), f32),
            jax.ShapeDtypeStruct((2, 128, HD), f32),
            jax.ShapeDtypeStruct((2, 128, HD), f32),
        ),
        in_specs=[smem] * 2 + [vmem] * 8,
        out_specs=(vmem,) * 4,
        scratch_shapes=[
            pltpu.VMEM((8 * FEAT, TOK), bf16),
            pltpu.VMEM((HROWS, TOK), bf16),
            pltpu.VMEM((NBLK, HD, 128), bf16),
            pltpu.VMEM((2, TOK, HD), bf16),
            pltpu.VMEM((HROWS, HD), f32),
            pltpu.VMEM((8, HALF + 1, 8, HD), i32),
            pltpu.VMEM((8, HALF + 1, 8, HD), i32),
            pltpu.VMEM((PAD, SUB, HD), f32),
            pltpu.VMEM((8, OWN + 1, 8, HD), i32),
            pltpu.VMEM((8, OWN + 1, 8, HD), i32),
            pltpu.VMEM((OWN, SUB, HD), f32),
            pltpu.VMEM((64, 8, HD), i32),
            pltpu.VMEM((8, 6, 8, HD), i32),
            pltpu.VMEM((48, 8, HD), i32),
            pltpu.VMEM((8, 3 * OWN, 8, HD), i32),
            pltpu.VMEM((8 * 3 * OWN, 8, HD), i32),
            pltpu.VMEM((8, 2, SUB, HD), f32),
            pltpu.VMEM((8, 2, SUB, HD), f32),
        ]
        + pair(CHUNKS, 2)
        + pair(3, CHUNKS)
        + pair(3, CHUNKS, 2)
        + pair(CHUNKS)
        + pair(CHUNKS)
        + pair(7)
        + pair(7)
        + pair(7)
        + pair(7)
        + pair(7)
        + pair(3, 8)
        + pair(4, 8)
        + pair(7)
        + pair(7)
        + [dma],
        compiler_params=pltpu.CompilerParams(
            collective_id=0, has_side_effects=True, vmem_limit_bytes=56 * 2**20
        ),
        name="project_back",
    )(
        slot_code, block_code,
        activation.T, w_query.reshape(NBLK, 128, HD), key_rows, value_rows, out_grad,
        master_copy, first_moment, second_moment,
    )
    return (new_w.reshape(PAD * 128, HD)[: NBLK * 128], new_m, new_f, new_s)


def solution(mesh):
    return jax.shard_map(
        body,
        mesh=mesh,
        in_specs=(
            P("dp", "tensor"),
            P(None, "tensor"),
            P("dp", "tensor"),
            P("dp", "tensor"),
            P("dp", "tensor"),
            P("tensor", None, None),
            P("dp", None, "tensor"),
            P("dp", None, "tensor"),
            P("dp", None, "tensor"),
        ),
        out_specs=(
            P(None, "tensor"),
            P("dp", None, "tensor"),
            P("dp", None, "tensor"),
            P("dp", None, "tensor"),
        ),
        check_vma=False,
    )
```

time: 215 us -> 158 us (0.73)
  the two profiles are of different devices: /device:TPU:97 before, /device:TPU:1 now
where the time goes in v2:
time: 158 us; the launch traced here: 156 us
  Pallas kernels  148 us (94%)
  local copies, waits for them, and re-layouts  5.38 us (3%)
  other arithmetic  2.1 us (1%)
    pallas_call x1, Pallas kernels, body(): pl.pallas_call(kernel, out_shape=(jax.ShapeDtypeStruct((PAD, 128, HD), bf...  148 us

profile of v2, /device:TPU:1, one launch (start us, length us, event | category | flops | bytes accessed | tf_op | source)
XLA Modules:
  0.0 155.9 jit_solution(9404989419756975908)
XLA Ops:
  0.6 0.8 convert_reduce_fusion
  1.5 0.7 fusion.6
  2.1 0.5 pad.4.block_code
  2.6 0.6 select_reduce_fusion.slot_code
  3.2 147.7 %project_back.1 = (bf16[56,128,128]{2,1,0:T(8,128)(2,1)}, f32[2,128,128]{2,1,0:T(8,128)}, f32[2,128,128]{2,1,0:T(8,128)}, f32[2,128,128]{2,1,0:T(8,128)}) custom-call(s32[128]{0:T(128)} %select_reduce_fusion.slot_code, s32[56]{0:T(128)} %pad.4.block_code, bf16[832,384]{1,0:T(8,128)(2,1)} %bitcast.8, bf16[52,128,128]{2,1,0:T(8,128)(2,1)} %bitcast.6, ...), custom_call_target="tpu_custom_call" | custom-call | tf_op jit(solution)/shard_map/project_back/pallas_call | solution.py:428
  151.0 0.0 copy-start.2
  151.0 0.0 copy-start.1
  151.0 0.0 copy-start
  151.0 2.9 %slice.6 = bf16[52,128,128]{2,1,0:T(8,128)(2,1)} slice(bf16[56,128,128]{2,1,0:T(8,128)(2,1)} %get-tuple-element.8), slice={[0:52], [0:128], [0:128]} | slice | bytes 3407872 | tf_op jit(solution)/shard_map/slice | solution.py:482
  153.9 0.0 copy-done.2
  153.9 0.7 copy.16
  154.5 0.0 copy-done.1
  154.5 0.7 copy.17
  155.2 0.0 copy-done
  155.2 0.7 copy.18
Async XLA Ops:
  151.0 2.9 %copy-start.2 = (f32[2,128,128]{2,1,0:T(8,128)S(1)}, f32[2,128,128]{2,1,0:T(8,128)}, u32[]{:S(2)}) copy-start(f32[2,128,128]{2,1,0:T(8,128)} %get-tuple-element.20) | copy-start | bytes 393220
  151.0 3.6 %copy-start.1 = (f32[2,128,128]{2,1,0:T(8,128)S(1)}, f32[2,128,128]{2,1,0:T(8,128)}, u32[]{:S(2)}) copy-start(f32[2,128,128]{2,1,0:T(8,128)} %get-tuple-element.21) | copy-start | bytes 393220
  151.0 4.2 %copy-start = (f32[2,128,128]{2,1,0:T(8,128)S(1)}, f32[2,128,128]{2,1,0:T(8,128)}, u32[]{:S(2)}) copy-start(f32[2,128,128]{2,1,0:T(8,128)} %get-tuple-element.22) | copy-start | bytes 393220

commit v3 on v2

v3 whole, which is shorter than its diff:
```python
import functools

import jax
import jax.numpy as jnp
from jax import lax
from jax.experimental import pallas as pl
from jax.experimental.pallas import tpu as pltpu
from jax.sharding import PartitionSpec as P

beta_first = 0.9
beta_second = 0.95
learn_rate = 0.001
adam_eps = 1e-08
adam_step = 100.0

MESH = pl.DeviceIdType.MESH
TOK = 384
FEAT = 832
HD = 128
NBLK = 52
HALF = 26
HROWS = HALF * 128
SUB = 16
OWN = 7
PAD = 8 * OWN
CHUNKS = 3
CTOK = TOK // CHUNKS
LEVELS = 32700.0
FIXED = 32766.0
TOP_MASTER = 0.078125
TOP_FIRST = 4.0
TOP_SECOND = 1.0


def adam_update(gradient, master, first, second, used):
    first_new = beta_first * first + (1.0 - beta_first) * gradient
    second_new = beta_second * second + (1.0 - beta_second) * gradient * gradient
    corr_first = 1.0 - beta_first**adam_step
    corr_second = 1.0 - beta_second**adam_step
    master_new = master - learn_rate * (first_new / corr_first) / (
        jnp.sqrt(second_new / corr_second) + adam_eps
    )
    return (master_new * used, first_new * used, second_new * used)


def dot_t(a, b):
    return lax.dot_general(a, b, (((1,), (1,)), ((), ())), preferred_element_type=jnp.float32)


def dot_0(a, b):
    return lax.dot_general(a, b, (((0,), (0,)), ((), ())), preferred_element_type=jnp.float32)


def pack(v, inv):
    q = jnp.round(v * inv).astype(jnp.int32)
    return (q[:8] << 16) | (q[8:] & 0xFFFF)


def unpack(u, step):
    return jnp.concatenate([u >> 16, (u << 16) >> 16], axis=0).astype(jnp.float32) * step


def level(top):
    bits = jnp.log(jnp.maximum(top, 1e-30)) * (8.0 / 0.6931471805599453)
    return jnp.ceil(bits).astype(jnp.int32)


def step_of(e):
    return jnp.exp(e.astype(jnp.float32) * (0.6931471805599453 / 8.0)) * (1.0 / LEVELS)


def inverse_of(e):
    return jnp.exp(e.astype(jnp.float32) * (-0.6931471805599453 / 8.0)) * LEVELS


def kernel(
    slot_code, block_code,
    act, w, keys, values, outg, master, first, second,
    out_w, out_m, out_f, out_s,
    whole, sib, wt, wo, qo, po, pr, dqs, dqa, grad, ys, yr, gsum, zs, zr, red, gq,
    sys, syr, szs, szr, wst, send_g, recv_g,
    x_s, x_r, s_s, s_r, b_s, b_r, q_s, q_r, h_s, h_r, d_s, d_r, y_s, y_r, r_s, r_r,
    a_s, a_r, o_s, o_r, w_s, w_r, v_s, v_r, c_s, c_r, k_s, k_r, p_s, p_r, l_sem,
):
    dp = lax.axis_index("dp")
    t = lax.axis_index("tensor")
    zl = dp // 8
    part = lax.rem(dp, 8)
    y = part // 2
    c = lax.rem(part, 2)
    a = t // 4
    x = lax.rem(t, 4)
    f32 = jnp.float32
    bf16 = jnp.bfloat16

    def device(z, y, c, a):
        return (z * 8 + y * 2 + c, a * 4 + x)

    def at_x(d):
        return (dp, a * 4 + lax.rem(x + d, 4))

    def at_part(p):
        return (zl * 8 + p, t)

    def at_z(z):
        return (z * 8 + part, t)

    opposite = device(zl, y, c, 1 - a)
    sibling = device(zl, y, 1 - c, a)

    def rows(start, n, unit):
        return pl.ds(pl.multiple_of(start, unit), n)

    barrier = pltpu.get_barrier_semaphore()
    peers = [at_x(d) for d in (1, 2, 3)] + [opposite]
    peers += [at_part(lax.rem(part + d, 8)) for d in range(1, 8)]
    peers += [at_z(lax.rem(zl + d, 8)) for d in range(1, 8)]
    peers += [device(lax.rem(zl + d, 8), y, 1 - c, 1 - a) for d in range(8)]
    for peer in peers:
        pl.semaphore_signal(barrier, inc=1, device_id=peer, device_id_type=MESH)

    def turn(k, carry):
        wt[rows(k * 128, 128, 128)] = w[k].astype(f32).T.astype(bf16)
        return carry

    lax.fori_loop((1 - a) * HALF, (1 - a) * HALF + HALF, turn, 0)
    pl.semaphore_wait(barrier, len(peers))
    sent = []

    def copy(src, dst, ss, rs, dev):
        return pltpu.make_async_remote_copy(
            src_ref=src, dst_ref=dst, send_sem=ss, recv_sem=rs, device_id=dev, device_id_type=MESH
        )

    def go(src, dst, ss, rs, dev):
        cp = copy(src, dst, ss, rs, dev)
        cp.start()
        sent.append(cp)
        return cp

    eighth = rows(part * 416, 416, 16)
    w_cross = go(
        wt.at[rows((1 - a) * HROWS + part * 416, 416, 16)], wo.at[eighth],
        b_s.at[0], b_r.at[0], opposite,
    )

    cols = [pl.ds(i * CTOK, CTOK) for i in range(CHUNKS)]
    mine = rows(x * FEAT, FEAT, 16)
    own = pltpu.make_async_copy(act, whole.at[mine], l_sem)
    own.start()
    along = [
        [
            go(act.at[:, cols[i]], whole.at[mine, cols[i]], x_s.at[d - 1, i], x_r.at[d - 1, i], at_x(d))
            for d in (1, 3, 2)
        ]
        for i in range(CHUNKS)
    ]

    def states(p, carry):
        for j in range(2):
            for s in range(2):
                r = rows((p // 2) * 32 + s * SUB, SUB, SUB)
                n = j * 2 + s
                sys[p, n] = pack(master[j, r], FIXED / TOP_MASTER)
                sys[p, 4 + n] = pack(first[j, r], FIXED / TOP_FIRST)
                sys[p, 8 + n] = pack(second[j, r], FIXED / TOP_SECOND)
        return carry

    lax.fori_loop(0, 8, states, 0)
    state_y = []
    for d in range(1, 8):
        p = lax.rem(part + d, 8)
        state_y.append(
            go(sys.at[p], syr.at[pl.ds(part * 12, 12)], k_s.at[d - 1], k_r.at[d - 1], at_part(p))
        )
    syr[pl.ds(part * 12, 12)] = sys[part]
    lax.fori_loop(a * HALF, a * HALF + HALF, turn, 0)
    for cp in state_y:
        cp.wait_recv()

    def states_z(z, carry):
        for j in range(OWN):
            u = z * OWN + j
            at = (block_code[c * HALF + u // 2] & 127) + lax.rem(u, 2)
            for m in range(3):
                szs[m, z, j] = syr[at + 4 * m]
        return carry

    lax.fori_loop(0, 8, states_z, 0)
    state_z = []

    def send_states(m):
        szr[m, pl.ds(zl * OWN, OWN)] = szs[m, zl]
        for d in range(1, 8):
            z = lax.rem(zl + d, 8)
            state_z.append(
                go(
                    szs.at[m, z], szr.at[m, pl.ds(zl * OWN, OWN)],
                    p_s.at[m, d - 1], p_r.at[m, d - 1], at_z(z),
                )
            )

    send_states(0)
    send_states(1)
    w_cross.wait_recv()
    w_part = []
    for d in range(1, 8):
        p = lax.rem(part + d, 8)
        w_part.append(go(wo.at[eighth], wo.at[eighth], b_s.at[d], b_r.at[d], at_part(p)))

    def partial(weights, first_row, i):
        def add_q(k, total):
            for m in range(13):
                n = k * 13 + m
                total = total + jnp.dot(
                    weights[rows(first_row + n * 128, 128, 128)],
                    whole[rows(n * 128, 128, 128), cols[i]],
                    preferred_element_type=f32,
                )
            return total

        return lax.fori_loop(0, 2, add_q, jnp.zeros((HD, CTOK), f32))

    own.wait()
    share = []
    for i in range(CHUNKS):
        for cp in along[i]:
            cp.wait_recv()
        share.append(go(whole.at[:, cols[i]], sib.at[:, cols[i]], s_s.at[i], s_r.at[i], sibling))
        qo[i] = partial(wt, a * HROWS, i)
    for cp in w_part:
        cp.wait_recv()
    q_cross = []
    for i in range(CHUNKS):
        po[i] = partial(wo, 0, i)
        q_cross.append(go(po.at[i], pr.at[i], q_s.at[i], q_r.at[i], opposite))

    factor = HD ** (-0.5)
    same = a == c
    dq_cross = []
    for i in range(CHUNKS):
        q_cross[i].wait_recv()
        queries = (qo[i] + pr[i]).T.astype(bf16)
        n = (i + 1) * CTOK
        kk = keys[pl.ds(0, n)]
        vv = values[pl.ds(0, n)]
        og = outg[cols[i]]
        scores = dot_t(queries, kk) * factor
        row_pos = lax.broadcasted_iota(jnp.int32, (CTOK, n), 0) + i * CTOK
        col_pos = lax.broadcasted_iota(jnp.int32, (CTOK, n), 1)
        scores = jnp.where(row_pos >= col_pos, scores, -1e30)
        shifted = jnp.exp(scores - jnp.max(scores, axis=1, keepdims=True))
        attention = shifted / jnp.sum(shifted, axis=1, keepdims=True)
        outputs = jnp.dot(attention.astype(bf16), vv, preferred_element_type=f32)
        deltas = jnp.sum(og.astype(f32) * outputs, axis=1, keepdims=True)
        upstream = dot_t(og, vv)
        dscores = (attention * (upstream - deltas)).astype(bf16)
        dquery = jnp.dot(dscores, kk, preferred_element_type=f32) * factor
        dqs[cols[i]] = dquery.astype(bf16)
        go(
            dqs.at[cols[i]], dqa.at[c, cols[i]], d_s.at[i], d_r.at[i, c], device(zl, y, a, 1 - a)
        )

        @pl.when(same)
        def _():
            dqa[c, cols[i]] = dqs[cols[i]]

        @pl.when(jnp.logical_not(same))
        def _():
            copy(dqs.at[cols[i]], dqa.at[c, cols[i]], h_s.at[i], h_r.at[i], sibling).start()

    send_states(2)

    def wait_dq(i):
        @pl.when(same)
        def _():
            copy(dqs.at[cols[i]], dqa.at[1 - c, cols[i]], h_s.at[i], h_r.at[i], sibling).wait_recv()

        @pl.when(jnp.logical_not(same))
        def _():
            for s in range(2):
                copy(
                    dqs.at[cols[i]], dqa.at[s, cols[i]], d_s.at[i], d_r.at[i, s], opposite
                ).wait_recv()
            copy(dqs.at[cols[i]], dqa.at[c, cols[i]], h_s.at[i], h_r.at[i], sibling).wait_send()

    def add_grad(lo, n, fresh):
        tok = pl.ds(lo, n)

        def one(j, top):
            r = rows(j * FEAT, FEAT, 16)
            g = jnp.dot(whole[r, tok], dqa[c, tok], preferred_element_type=f32)
            g = g + jnp.dot(sib[r, tok], dqa[1 - c, tok], preferred_element_type=f32)
            if not fresh:
                g = g + grad[r]
            grad[r] = g
            return jnp.maximum(top, jnp.max(jnp.abs(g), axis=0, keepdims=True))

        return lax.fori_loop(0, 4, one, jnp.zeros((1, HD), f32))

    for cp in share:
        cp.wait_recv()
    wait_dq(0)
    wait_dq(1)
    add_grad(0, 2 * CTOK, True)
    wait_dq(2)
    top = add_grad(2 * CTOK, CTOK, False)

    e = jnp.broadcast_to(level(top), (8, HD))
    inv = inverse_of(e[:1])

    def to_fixed(b, carry):
        for p in range(4):
            for s in range(2):
                ys[p, b * 2 + s] = pack(grad[rows(b * 128 + p * 32 + s * SUB, SUB, SUB)], inv)
        return carry

    lax.fori_loop(0, HALF, to_fixed, 0)
    for p in range(4):
        ys[p, NBLK] = e
    to_y = []
    for d in (1, 3, 2):
        p = lax.rem(y + d, 4)
        to_y.append(go(ys.at[p], yr.at[y], y_s.at[d - 1], y_r.at[d - 1], device(zl, p, c, a)))
    yr[y] = ys[y]
    for cp in to_y:
        cp.wait_recv()
    steps = [step_of(yr[p, NBLK, 0:1]) for p in range(4)]

    def add_y(b, top):
        for s in range(2):
            u = b * 2 + s
            total = unpack(yr[0, u], steps[0])
            for p in range(1, 4):
                total = total + unpack(yr[p, u], steps[p])
            gsum[u] = total
            top = jnp.maximum(top, jnp.max(jnp.abs(total), axis=0, keepdims=True))
        return top

    top = lax.fori_loop(0, HALF, add_y, jnp.zeros((1, HD), f32))
    gsum[pl.ds(NBLK, PAD - NBLK)] = jnp.zeros((PAD - NBLK, SUB, HD), f32)

    e = jnp.broadcast_to(level(top), (8, HD))
    inv = inverse_of(e[:1])

    def to_fixed_z(z, carry):
        for j in range(OWN):
            zs[z, j] = pack(gsum[z * OWN + j], inv)
        zs[z, OWN] = e
        return carry

    lax.fori_loop(0, 8, to_fixed_z, 0)
    to_z = []
    for d in range(1, 8):
        z = lax.rem(zl + d, 8)
        to_z.append(go(zs.at[z], zr.at[zl], r_s.at[d], r_r.at[d], device(z, y, a, c)))
    turned = copy(zs.at[zl], zr.at[zl], r_s.at[0], r_r.at[0], device(zl, y, 1 - c, 1 - a))

    @pl.when(same)
    def _():
        zr[zl] = zs[zl]

    @pl.when(jnp.logical_not(same))
    def _():
        turned.start()
        turned.wait()

    for cp in to_z + state_z:
        cp.wait_recv()
    steps = [step_of(zr[z, OWN, 0:1]) for z in range(8)]
    top = jnp.zeros((1, HD), f32)
    for j in range(OWN):
        total = unpack(zr[0, j], steps[0])
        for z in range(1, 8):
            total = total + unpack(zr[z, j], steps[z])
        red[j] = total
        top = jnp.maximum(top, jnp.max(jnp.abs(total), axis=0, keepdims=True))
        u = zl * OWN + j
        at = (block_code[c * HALF + u // 2] >> 7) + j
        m_state = unpack(szr[0, at], TOP_MASTER / FIXED)
        f_state = unpack(szr[1, at], TOP_FIRST / FIXED)
        s_state = unpack(szr[2, at], TOP_SECOND / FIXED)
        nm, _, _ = adam_update(total, m_state, f_state, s_state, 1.0)
        wst[part, u] = nm.astype(bf16)

    def weights(z, p):
        return wst.at[p, pl.ds(z * OWN, OWN)]

    w_z = []
    for d in range(1, 8):
        z = lax.rem(zl + d, 8)
        w_z.append(go(weights(zl, part), weights(zl, part), w_s.at[d - 1], w_r.at[d - 1], at_z(z)))
    e = jnp.broadcast_to(level(top), (8, HD))
    inv = inverse_of(e[:1])
    for j in range(OWN):
        gq[zl * 8 + j] = pack(red[j], inv)
    gq[zl * 8 + OWN] = e
    g_z = []
    for d in range(1, 8):
        z = lax.rem(zl + d, 8)
        at = gq.at[pl.ds(zl * 8, 8)]
        g_z.append(go(at, at, a_s.at[d - 1], a_r.at[d - 1], at_z(z)))

    back_y = []
    to_core = []
    for d in range(8):
        z = lax.rem(zl - d + 8, 8)
        if d:
            w_z[d - 1].wait_recv()
        at = weights(z, part)
        back_y.append(
            [
                go(at, at, v_s.at[q - 1, d], v_r.at[q - 1, d], device(zl, lax.rem(y + q, 4), c, a))
                for q in (1, 3, 2)
            ]
        )
        to_core.append(go(at, at, c_s.at[0, d], c_r.at[0, d], sibling))

    for cp in g_z:
        cp.wait_recv()
    for p in range(8):
        for j in range(2):
            code = slot_code[zl * 16 + p * 2 + j]
            for s in range(2):
                u = (code >> (6 * s)) & 63
                send_g[p, j * 2 + s] = unpack(gq[u], step_of(gq[u | OWN][:1]))
    to_owner = []
    for d in range(1, 8):
        p = lax.rem(part + d, 8)
        to_owner.append(
            go(send_g.at[p], recv_g.at[pl.ds(part * 4, 4)], o_s.at[d - 1], o_r.at[d - 1], at_part(p))
        )
    recv_g[pl.ds(part * 4, 4)] = send_g[part]
    for d in range(8):
        z = lax.rem(zl - d + 8, 8)
        for n, q in enumerate((1, 3, 2)):
            back_y[d][n].wait_recv()
            at = weights(z, lax.rem(y - q + 4, 4) * 2 + c)
            to_core.append(go(at, at, c_s.at[q, d], c_r.at[q, d], sibling))
    for cp in to_owner:
        cp.wait_recv()
    for j in range(2):
        code = slot_code[dp * 2 + j]
        used = (code >> 13).astype(f32)
        h = ((code >> 12) & 1) * 4
        for n in range(4):
            for s in range(2):
                g = recv_g[h + (n * 8 + j * 2 + s)]
                r = pl.ds(n * 32 + s * SUB, SUB)
                nm, nf, ns = adam_update(g, master[j, r], first[j, r], second[j, r], used)
                out_m[j, r] = nm
                out_f[j, r] = nf
                out_s[j, r] = ns
    for cp in to_core:
        cp.wait_recv()

    def place(b, carry):
        for p in range(8):
            for s in range(2):
                out_w[(p % 2) * HALF + b, (p // 2) * 32 + s * SUB : (p // 2) * 32 + (s + 1) * SUB] = wst[p, b * 2 + s]
        return carry

    lax.fori_loop(0, HALF, place, 0)
    for cp in sent:
        cp.wait_send()


def body(
    activation, w_query, key_rows, value_rows, out_grad, owners, master_copy, first_moment, second_moment
):
    own_row = owners[0, :, 0]
    order = jnp.arange(NBLK, dtype=jnp.int32)
    earlier = (own_row[:, None] == own_row[None, :]) & (order[:, None] < order[None, :])
    second_slot = jnp.sum(earlier.astype(jnp.int32), axis=0)
    target = own_row * 2 + second_slot
    match = target[None, :] == jnp.arange(128, dtype=jnp.int32)[:, None]
    unit = (order % HALF) * 2
    place = (unit // OWN) * 8 + unit % OWN
    place = place + 64 * (((unit + 1) // OWN) * 8 + (unit + 1) % OWN)
    place = place + 4096 * (order // HALF) + 8192
    slot_code = jnp.sum(jnp.where(match, place[None, :], 0), axis=1)
    block_code = (own_row // 8) * (OWN * 128) + (own_row % 8) * 12 + second_slot * 2
    block_code = jnp.pad(block_code, (0, PAD - NBLK))
    smem = pl.BlockSpec(memory_space=pltpu.SMEM)
    vmem = pl.BlockSpec(memory_space=pltpu.VMEM)
    f32 = jnp.float32
    bf16 = jnp.bfloat16
    i32 = jnp.int32
    dma = pltpu.SemaphoreType.DMA

    def pair(*dims):
        return [dma(dims), dma(dims)]

    new_w, new_m, new_f, new_s = pl.pallas_call(
        kernel,
        out_shape=(
            jax.ShapeDtypeStruct((NBLK, 128, HD), bf16),
            jax.ShapeDtypeStruct((2, 128, HD), f32),
            jax.ShapeDtypeStruct((2, 128, HD), f32),
            jax.ShapeDtypeStruct((2, 128, HD), f32),
        ),
        in_specs=[smem] * 2 + [vmem] * 8,
        out_specs=(vmem,) * 4,
        scratch_shapes=[
            pltpu.VMEM((HROWS, TOK), bf16),
            pltpu.VMEM((HROWS, TOK), bf16),
            pltpu.VMEM((2 * HROWS, 128), bf16),
            pltpu.VMEM((HROWS, 128), bf16),
            pltpu.VMEM((CHUNKS, HD, CTOK), f32),
            pltpu.VMEM((CHUNKS, HD, CTOK), f32),
            pltpu.VMEM((CHUNKS, HD, CTOK), f32),
            pltpu.VMEM((TOK, HD), bf16),
            pltpu.VMEM((2, TOK, HD), bf16),
            pltpu.VMEM((HROWS, HD), f32),
            pltpu.VMEM((4, NBLK + 1, 8, HD), i32),
            pltpu.VMEM((4, NBLK + 1, 8, HD), i32),
            pltpu.VMEM((PAD, SUB, HD), f32),
            pltpu.VMEM((8, OWN + 1, 8, HD), i32),
            pltpu.VMEM((8, OWN + 1, 8, HD), i32),
            pltpu.VMEM((OWN, SUB, HD), f32),
            pltpu.VMEM((64, 8, HD), i32),
            pltpu.VMEM((8, 12, 8, HD), i32),
            pltpu.VMEM((96, 8, HD), i32),
            pltpu.VMEM((3, 8, OWN, 8, HD), i32),
            pltpu.VMEM((3, PAD, 8, HD), i32),
            pltpu.VMEM((8, PAD, SUB, HD), bf16),
            pltpu.VMEM((8, 4, SUB, HD), f32),
            pltpu.VMEM((32, SUB, HD), f32),
        ]
        + pair(3, CHUNKS)
        + pair(CHUNKS)
        + pair(8)
        + pair(CHUNKS)
        + pair(CHUNKS)
        + [dma((CHUNKS,)), dma((CHUNKS, 2))]
        + pair(3)
        + pair(8)
        + pair(7)
        + pair(7)
        + pair(7)
        + pair(3, 8)
        + pair(4, 8)
        + pair(7)
        + pair(3, 7)
        + [dma],
        compiler_params=pltpu.CompilerParams(
            collective_id=0, has_side_effects=True, vmem_limit_bytes=56 * 2**20
        ),
        name="project_back",
    )(
        slot_code, block_code,
        activation.T, w_query.reshape(NBLK, 128, HD), key_rows, value_rows, out_grad,
        master_copy, first_moment, second_moment,
    )
    return (new_w.reshape(NBLK * 128, HD), new_m, new_f, new_s)


def solution(mesh):
    return jax.shard_map(
        body,
        mesh=mesh,
        in_specs=(
            P("dp", "tensor"),
            P(None, "tensor"),
            P("dp", "tensor"),
            P("dp", "tensor"),
            P("dp", "tensor"),
            P("tensor", None, None),
            P("dp", None, "tensor"),
            P("dp", None, "tensor"),
            P("dp", None, "tensor"),
        ),
        out_specs=(
            P(None, "tensor"),
            P("dp", None, "tensor"),
            P("dp", None, "tensor"),
            P("dp", None, "tensor"),
        ),
        check_vma=False,
    )
```

time: 158 us -> 145 us (0.918); the launches traced: 156 us -> 145 us
  Pallas kernels: 148 us -> 137 us
    pallas_call x1, Pallas kernels: 148 us -> 137 us  [body(): pl.pallas_call(kernel, out_shape=(jax.ShapeDtypeStruct((NBLK, 128, HD), b...]
    slice x1 -> x0, local copies, waits for them, and re-layouts: 2.89 us -> none  [body(): return (new_w.reshape(PAD * 128, HD)[:NBLK * 128], new_m, new_f, new_s)]
    unnamed x9 -> x10, local copies, waits for them, and re-layouts: 1.98 us -> 4.78 us
where the time goes in v3:
time: 145 us
  Pallas kernels  137 us (94%)
  local copies, waits for them, and re-layouts  5.29 us (4%)
  other arithmetic  2.12 us (1%)
    pallas_call x1, Pallas kernels, body(): pl.pallas_call(kernel, out_shape=(jax.ShapeDtypeStruct((NBLK, 128, HD), b...  137 us
    unnamed x10, local copies, waits for them, and re-layouts  4.78 us

profile of v3, /device:TPU:1, one launch (start us, length us, event | category | flops | bytes accessed | tf_op | source)
XLA Modules:
  0.0 145.2 jit_solution(6593320754794080212)
XLA Ops:
  0.6 0.8 convert_reduce_fusion
  1.5 0.7 fusion.10
  2.1 0.5 pad.4.block_code
  2.7 0.6 select_reduce_fusion.slot_code
  3.3 137.1 %project_back.1 = (bf16[52,128,128]{2,1,0:T(8,128)(2,1)}, f32[2,128,128]{2,1,0:T(8,128)}, f32[2,128,128]{2,1,0:T(8,128)}, f32[2,128,128]{2,1,0:T(8,128)}) custom-call(s32[128]{0:T(128)} %select_reduce_fusion.slot_code, s32[56]{0:T(128)} %pad.4.block_code, bf16[832,384]{1,0:T(8,128)(2,1)} %bitcast.8, bf16[52,128,128]{2,1,0:T(8,128)(2,1)} %bitcast.6, ...), custom_call_target="tpu_custom_call" | custom-call | tf_op jit(solution)/shard_map/project_back/pallas_call | solution.py:494
  140.4 0.0 copy-start.2
  140.4 0.0 copy-start.1
  140.4 0.0 copy-start
  140.4 2.8 %copy.17 = bf16[6656,128]{1,0:T(8,128)(2,1)} copy(bf16[6656,128]{1,0:T(8,128)(2,1)} %bitcast.7) | data formatting | bytes 3407872
  143.2 0.0 copy-done.2
  143.2 0.7 copy.18
  143.9 0.0 copy-done.1
  143.9 0.7 copy.19
  144.6 0.0 copy-done
  144.6 0.7 copy.20
Async XLA Ops:
  140.4 2.8 %copy-start.2 = (f32[2,128,128]{2,1,0:T(8,128)S(1)}, f32[2,128,128]{2,1,0:T(8,128)}, u32[]{:S(2)}) copy-start(f32[2,128,128]{2,1,0:T(8,128)} %get-tuple-element.20) | copy-start | bytes 393220
  140.4 3.5 %copy-start.1 = (f32[2,128,128]{2,1,0:T(8,128)S(1)}, f32[2,128,128]{2,1,0:T(8,128)}, u32[]{:S(2)}) copy-start(f32[2,128,128]{2,1,0:T(8,128)} %get-tuple-element.21) | copy-start | bytes 393220
  140.4 4.1 %copy-start = (f32[2,128,128]{2,1,0:T(8,128)S(1)}, f32[2,128,128]{2,1,0:T(8,128)}, u32[]{:S(2)}) copy-start(f32[2,128,128]{2,1,0:T(8,128)} %get-tuple-element.22) | copy-start | bytes 393220

commit v4 on v3

--- a/solution.py
+++ b/solution.py
@@ -26,6 +26,7 @@
 CHUNKS = 3
 CTOK = TOK // CHUNKS
 LEVELS = 32700.0
+FINE = 8388000.0
 FIXED = 32766.0
 TOP_MASTER = 0.078125
 TOP_FIRST = 4.0
@@ -53,11 +54,30 @@
 
 def pack(v, inv):
     q = jnp.round(v * inv).astype(jnp.int32)
-    return (q[:8] << 16) | (q[8:] & 0xFFFF)
+    k = q.shape[0] // 2
+    return (q[:k] << 16) | (q[k:] & 0xFFFF)
 
 
 def unpack(u, step):
     return jnp.concatenate([u >> 16, (u << 16) >> 16], axis=0).astype(jnp.float32) * step
+
+
+def pack_fine(v, inv):
+    q = jnp.round(v * inv).astype(jnp.int32)
+    last = q[96:]
+    return jnp.concatenate(
+        [
+            (q[0:32] << 8) | (last & 255),
+            (q[32:64] << 8) | ((last >> 8) & 255),
+            (q[64:96] << 8) | ((last >> 16) & 255),
+        ],
+        axis=0,
+    )
+
+
+def unpack_fine(u, step):
+    last = ((u[64:96] << 24) >> 8) | ((u[32:64] & 255) << 8) | (u[0:32] & 255)
+    return jnp.concatenate([u >> 8, last], axis=0).astype(jnp.float32) * step
 
 
 def level(top):
@@ -76,10 +96,10 @@
 def kernel(
     slot_code, block_code,
     act, w, keys, values, outg, master, first, second,
-    out_w, out_m, out_f, out_s,
-    whole, sib, wt, wo, qo, po, pr, dqs, dqa, grad, ys, yr, gsum, zs, zr, red, gq,
-    sys, syr, szs, szr, wst, send_g, recv_g,
-    x_s, x_r, s_s, s_r, b_s, b_r, q_s, q_r, h_s, h_r, d_s, d_r, y_s, y_r, r_s, r_r,
+    wst, recv_g,
+    whole, sib, wt, wo, qo, po, pr, pm, pn, dqs, dqa, grad, ys, yr, gsum, zs, zr, red, gq,
+    sys, syr, szs, szr, send_g,
+    x_s, x_r, f_s, f_r, s_s, s_r, b_s, b_r, q_s, q_r, n_s, n_r, h_s, h_r, d_s, d_r, y_s, y_r, r_s, r_r,
     a_s, a_r, o_s, o_r, w_s, w_r, v_s, v_r, c_s, c_r, k_s, k_r, p_s, p_r, l_sem,
 ):
     dp = lax.axis_index("dp")
@@ -120,41 +140,12 @@
         pl.semaphore_signal(barrier, inc=1, device_id=peer, device_id_type=MESH)
 
     def turn(k, carry):
-        wt[rows(k * 128, 128, 128)] = w[k].astype(f32).T.astype(bf16)
+        r = rows(k * 128, 128, 128)
+        wt[r, 0:128] = w[k * 2].astype(f32).T.astype(bf16)
+        wt[r, 128:256] = w[k * 2 + 1].astype(f32).T.astype(bf16)
         return carry
 
-    lax.fori_loop((1 - a) * HALF, (1 - a) * HALF + HALF, turn, 0)
-    pl.semaphore_wait(barrier, len(peers))
-    sent = []
-
-    def copy(src, dst, ss, rs, dev):
-        return pltpu.make_async_remote_copy(
-            src_ref=src, dst_ref=dst, send_sem=ss, recv_sem=rs, device_id=dev, device_id_type=MESH
-        )
-
-    def go(src, dst, ss, rs, dev):
-        cp = copy(src, dst, ss, rs, dev)
-        cp.start()
-        sent.append(cp)
-        return cp
-
-    eighth = rows(part * 416, 416, 16)
-    w_cross = go(
-        wt.at[rows((1 - a) * HROWS + part * 416, 416, 16)], wo.at[eighth],
-        b_s.at[0], b_r.at[0], opposite,
-    )
-
-    cols = [pl.ds(i * CTOK, CTOK) for i in range(CHUNKS)]
-    mine = rows(x * FEAT, FEAT, 16)
-    own = pltpu.make_async_copy(act, whole.at[mine], l_sem)
-    own.start()
-    along = [
-        [
-            go(act.at[:, cols[i]], whole.at[mine, cols[i]], x_s.at[d - 1, i], x_r.at[d - 1, i], at_x(d))
-            for d in (1, 3, 2)
-        ]
-        for i in range(CHUNKS)
-    ]
+    lax.fori_loop(0, HALF, turn, 0)
 
     def states(p, carry):
         for j in range(2):
@@ -167,6 +158,48 @@
         return carry
 
     lax.fori_loop(0, 8, states, 0)
+    pl.semaphore_wait(barrier, len(peers))
+    sent = []
+
+    def copy(src, dst, ss, rs, dev):
+        return pltpu.make_async_remote_copy(
+            src_ref=src, dst_ref=dst, send_sem=ss, recv_sem=rs, device_id=dev, device_id_type=MESH
+        )
+
+    def go(src, dst, ss, rs, dev):
+        cp = copy(src, dst, ss, rs, dev)
+        cp.start()
+        sent.append(cp)
+        return cp
+
+    eighth = rows(part * 208, 208, 16)
+    w_cross = go(
+        wt.at[rows((1 - a) * (HROWS // 2) + part * 208, 208, 16)], wo.at[eighth],
+        b_s.at[0], b_r.at[0], opposite,
+    )
+
+    cols = [pl.ds(i * CTOK, CTOK) for i in range(CHUNKS)]
+    mine = rows(x * FEAT, FEAT, 16)
+    own = pltpu.make_async_copy(act, whole.at[mine], l_sem)
+    own.start()
+    order = (2, 1, 0)
+    along = {
+        i: [
+            go(act.at[:, cols[i]], whole.at[mine, cols[i]], x_s.at[n, i], x_r.at[n, i], at_x(d))
+            for n, d in enumerate((1, 3))
+        ]
+        for i in order
+    }
+    onward = {}
+
+    def pass_on(i):
+        onward[i] = []
+        for n, d in enumerate((1, 3)):
+            along[i][n].wait_recv()
+            r = rows(lax.rem(x - d + 4, 4) * FEAT + n * 416, 416, 16)
+            at = whole.at[r, cols[i]]
+            onward[i].append(go(at, at, f_s.at[n, i], f_r.at[n, i], at_x(d)))
+
     state_y = []
     for d in range(1, 8):
         p = lax.rem(part + d, 8)
@@ -174,14 +207,13 @@
             go(sys.at[p], syr.at[pl.ds(part * 12, 12)], k_s.at[d - 1], k_r.at[d - 1], at_part(p))
         )
     syr[pl.ds(part * 12, 12)] = sys[part]
-    lax.fori_loop(a * HALF, a * HALF + HALF, turn, 0)
     for cp in state_y:
         cp.wait_recv()
 
     def states_z(z, carry):
         for j in range(OWN):
             u = z * OWN + j
-            at = (block_code[c * HALF + u // 2] & 127) + lax.rem(u, 2)
+            at = (block_code[jnp.minimum(c * HALF + u // 2, NBLK - 1)] & 127) + lax.rem(u, 2)
             for m in range(3):
                 szs[m, z, j] = syr[at + 4 * m]
         return carry
@@ -202,45 +234,56 @@
 
     send_states(0)
     send_states(1)
+    pass_on(2)
+    pass_on(1)
     w_cross.wait_recv()
     w_part = []
     for d in range(1, 8):
         p = lax.rem(part + d, 8)
         w_part.append(go(wo.at[eighth], wo.at[eighth], b_s.at[d], b_r.at[d], at_part(p)))
+    pass_on(0)
 
     def partial(weights, first_row, i):
-        def add_q(k, total):
-            for m in range(13):
-                n = k * 13 + m
-                total = total + jnp.dot(
-                    weights[rows(first_row + n * 128, 128, 128)],
-                    whole[rows(n * 128, 128, 128), cols[i]],
-                    preferred_element_type=f32,
-                )
-            return total
-
-        return lax.fori_loop(0, 2, add_q, jnp.zeros((HD, CTOK), f32))
+        total = jnp.zeros((HD, CTOK), f32)
+        for n in range(13):
+            total = total + jnp.dot(
+                weights[rows(first_row + n * 128, 128, 128)],
+                whole[pl.ds(n * 256, 256), cols[i]],
+                preferred_element_type=f32,
+            )
+        return total
 
     own.wait()
     share = []
-    for i in range(CHUNKS):
-        for cp in along[i]:
+    q_cross = {}
+    grad[pl.ds(HROWS, 256)] = jnp.zeros((256, HD), f32)
+    for i in order:
+        for cp in onward[i]:
             cp.wait_recv()
         share.append(go(whole.at[:, cols[i]], sib.at[:, cols[i]], s_s.at[i], s_r.at[i], sibling))
-        qo[i] = partial(wt, a * HROWS, i)
-    for cp in w_part:
-        cp.wait_recv()
-    q_cross = []
-    for i in range(CHUNKS):
-        po[i] = partial(wo, 0, i)
-        q_cross.append(go(po.at[i], pr.at[i], q_s.at[i], q_r.at[i], opposite))
+        if i == order[0]:
+            qo[i] = partial(wt, a * (HROWS // 2), i)
+            for cp in w_part:
+                cp.wait_recv()
+        other = partial(wo, 0, i)
+        top = jnp.maximum(jnp.max(jnp.abs(other), axis=0, keepdims=True), 1e-30)
+        po[i] = pack_fine(other, FINE / top)
+        pm[i] = jnp.broadcast_to(top, (8, CTOK))
+        q_cross[i] = [
+            go(pm.at[i], pn.at[i], n_s.at[i], n_r.at[i], opposite),
+            go(po.at[i], pr.at[i], q_s.at[i], q_r.at[i], opposite),
+        ]
+    for i in order[1:]:
+        qo[i] = partial(wt, a * (HROWS // 2), i)
 
     factor = HD ** (-0.5)
     same = a == c
     dq_cross = []
-    for i in range(CHUNKS):
-        q_cross[i].wait_recv()
-        queries = (qo[i] + pr[i]).T.astype(bf16)
+    for i in order:
+        for cp in q_cross[i]:
+            cp.wait_recv()
+        other = unpack_fine(pr[i], pn[i, 0:1] * (1.0 / FINE))
+        queries = (qo[i] + other).T.astype(bf16)
         n = (i + 1) * CTOK
         kk = keys[pl.ds(0, n)]
         vv = values[pl.ds(0, n)]
@@ -300,72 +343,88 @@
 
     for cp in share:
         cp.wait_recv()
+    wait_dq(2)
+    wait_dq(1)
+    add_grad(CTOK, 2 * CTOK, True)
     wait_dq(0)
-    wait_dq(1)
-    add_grad(0, 2 * CTOK, True)
-    wait_dq(2)
-    top = add_grad(2 * CTOK, CTOK, False)
+    top = add_grad(0, CTOK, False)
 
     e = jnp.broadcast_to(level(top), (8, HD))
     inv = inverse_of(e[:1])
-
-    def to_fixed(b, carry):
+    to_y = []
+    for h in range(2):
+
+        def to_fixed(k, carry):
+            for j in range(OWN):
+                u = (2 * k + h) * OWN + j
+                r = (u // 2) * 128 + lax.rem(u, 2) * SUB
+                for p in range(4):
+                    ys[h, p, k * OWN + j] = pack(grad[rows(r + p * 32, SUB, SUB)], inv)
+            return carry
+
+        lax.fori_loop(0, 4, to_fixed, 0)
         for p in range(4):
-            for s in range(2):
-                ys[p, b * 2 + s] = pack(grad[rows(b * 128 + p * 32 + s * SUB, SUB, SUB)], inv)
-        return carry
-
-    lax.fori_loop(0, HALF, to_fixed, 0)
-    for p in range(4):
-        ys[p, NBLK] = e
-    to_y = []
-    for d in (1, 3, 2):
-        p = lax.rem(y + d, 4)
-        to_y.append(go(ys.at[p], yr.at[y], y_s.at[d - 1], y_r.at[d - 1], device(zl, p, c, a)))
-    yr[y] = ys[y]
-    for cp in to_y:
-        cp.wait_recv()
-    steps = [step_of(yr[p, NBLK, 0:1]) for p in range(4)]
-
-    def add_y(b, top):
-        for s in range(2):
-            u = b * 2 + s
-            total = unpack(yr[0, u], steps[0])
-            for p in range(1, 4):
-                total = total + unpack(yr[p, u], steps[p])
-            gsum[u] = total
-            top = jnp.maximum(top, jnp.max(jnp.abs(total), axis=0, keepdims=True))
-        return top
-
-    top = lax.fori_loop(0, HALF, add_y, jnp.zeros((1, HD), f32))
-    gsum[pl.ds(NBLK, PAD - NBLK)] = jnp.zeros((PAD - NBLK, SUB, HD), f32)
-
-    e = jnp.broadcast_to(level(top), (8, HD))
-    inv = inverse_of(e[:1])
-
-    def to_fixed_z(z, carry):
-        for j in range(OWN):
-            zs[z, j] = pack(gsum[z * OWN + j], inv)
-        zs[z, OWN] = e
-        return carry
-
-    lax.fori_loop(0, 8, to_fixed_z, 0)
-    to_z = []
-    for d in range(1, 8):
-        z = lax.rem(zl + d, 8)
-        to_z.append(go(zs.at[z], zr.at[zl], r_s.at[d], r_r.at[d], device(z, y, a, c)))
-    turned = copy(zs.at[zl], zr.at[zl], r_s.at[0], r_r.at[0], device(zl, y, 1 - c, 1 - a))
-
-    @pl.when(same)
-    def _():
-        zr[zl] = zs[zl]
-
-    @pl.when(jnp.logical_not(same))
-    def _():
-        turned.start()
-        turned.wait()
-
-    for cp in to_z + state_z:
+            ys[h, p, 4 * OWN] = e
+        for d in (1, 3, 2):
+            p = lax.rem(y + d, 4)
+            to_y.append(
+                go(ys.at[h, p], yr.at[h, y], y_s.at[h, d - 1], y_r.at[h, d - 1], device(zl, p, c, a))
+            )
+        yr[h, y] = ys[h, y]
+
+    def to_place(z):
+        return copy(zs.at[z], zr.at[zl], r_s.at[z], r_r.at[zl], device(z, y, a, c))
+
+    def from_place(z):
+        return copy(zs.at[z], zr.at[z], r_s.at[z], r_r.at[z], device(z, y, a, c))
+
+    def stays(z):
+        return jnp.logical_and(same, zl == z)
+
+    for h in range(2):
+        for cp in to_y[3 * h : 3 * h + 3]:
+            cp.wait_recv()
+        steps = [step_of(yr[h, p, 4 * OWN, 0:1]) for p in range(4)]
+
+        def add_y(k, top):
+            for j in range(OWN):
+                u = k * OWN + j
+                total = unpack(yr[h, 0, u], steps[0])
+                for p in range(1, 4):
+                    total = total + unpack(yr[h, p, u], steps[p])
+                gsum[u] = total
+                top = jnp.maximum(top, jnp.max(jnp.abs(total), axis=0, keepdims=True))
+            return top
+
+        top = lax.fori_loop(0, 4, add_y, jnp.zeros((1, HD), f32))
+        e = jnp.broadcast_to(level(top), (8, HD))
+        inv = inverse_of(e[:1])
+
+        def to_fixed_z(k, carry):
+            for j in range(OWN):
+                zs[2 * k + h, j] = pack(gsum[k * OWN + j], inv)
+            zs[2 * k + h, OWN] = e
+            return carry
+
+        lax.fori_loop(0, 4, to_fixed_z, 0)
+        for k in range(4):
+            z = 2 * k + h
+
+            @pl.when(stays(z))
+            def _():
+                zr[zl] = zs[z]
+
+            @pl.when(jnp.logical_not(stays(z)))
+            def _():
+                to_place(z).start()
+
+    for z in range(8):
+
+        @pl.when(jnp.logical_not(stays(z)))
+        def _():
+            from_place(z).wait_recv()
+
+    for cp in state_z:
         cp.wait_recv()
     steps = [step_of(zr[z, OWN, 0:1]) for z in range(8)]
     top = jnp.zeros((1, HD), f32)
@@ -376,7 +435,7 @@
         red[j] = total
         top = jnp.maximum(top, jnp.max(jnp.abs(total), axis=0, keepdims=True))
         u = zl * OWN + j
-        at = (block_code[c * HALF + u // 2] >> 7) + j
+        at = (block_code[jnp.minimum(c * HALF + u // 2, NBLK - 1)] >> 7) + j
         m_state = unpack(szr[0, at], TOP_MASTER / FIXED)
         f_state = unpack(szr[1, at], TOP_FIRST / FIXED)
         s_state = unpack(szr[2, at], TOP_SECOND / FIXED)
@@ -439,9 +498,30 @@
             to_core.append(go(at, at, c_s.at[q, d], c_r.at[q, d], sibling))
     for cp in to_owner:
         cp.wait_recv()
+    for cp in to_core:
+        cp.wait_recv()
+
+    for z in range(8):
+
+        @pl.when(jnp.logical_not(stays(z)))
+        def _():
+            to_place(z).wait_send()
+
+    for cp in sent:
+        cp.wait_send()
+
+
+def finish(slot_code, parts, recv, master, first, second, out_w, out_m, out_f, out_s, recv_g, sem):
+    moves = [pltpu.make_async_copy(recv, recv_g, sem.at[8])]
+    for p in range(8):
+        dst = out_w.at[pl.ds((p % 2) * HALF, HALF), pl.ds((p // 2) * 32, 32)]
+        moves.append(pltpu.make_async_copy(parts.at[p, pl.ds(0, HALF)], dst, sem.at[p]))
+    for cp in moves:
+        cp.start()
+    moves[0].wait()
     for j in range(2):
-        code = slot_code[dp * 2 + j]
-        used = (code >> 13).astype(f32)
+        code = slot_code[lax.axis_index("dp") * 2 + j]
+        used = (code >> 13).astype(jnp.float32)
         h = ((code >> 12) & 1) * 4
         for n in range(4):
             for s in range(2):
@@ -451,18 +531,8 @@
                 out_m[j, r] = nm
                 out_f[j, r] = nf
                 out_s[j, r] = ns
-    for cp in to_core:
-        cp.wait_recv()
-
-    def place(b, carry):
-        for p in range(8):
-            for s in range(2):
-                out_w[(p % 2) * HALF + b, (p // 2) * 32 + s * SUB : (p // 2) * 32 + (s + 1) * SUB] = wst[p, b * 2 + s]
-        return carry
-
-    lax.fori_loop(0, HALF, place, 0)
-    for cp in sent:
-        cp.wait_send()
+    for cp in moves[1:]:
+        cp.wait()
 
 
 def body(
@@ -480,9 +550,9 @@
     place = place + 4096 * (order // HALF) + 8192
     slot_code = jnp.sum(jnp.where(match, place[None, :], 0), axis=1)
     block_code = (own_row // 8) * (OWN * 128) + (own_row % 8) * 12 + second_slot * 2
-    block_code = jnp.pad(block_code, (0, PAD - NBLK))
     smem = pl.BlockSpec(memory_space=pltpu.SMEM)
     vmem = pl.BlockSpec(memory_space=pltpu.VMEM)
+    anywhere = pl.BlockSpec(memory_space=pl.ANY)
     f32 = jnp.float32
     bf16 = jnp.bfloat16
     i32 = jnp.int32
@@ -491,30 +561,30 @@
     def pair(*dims):
         return [dma(dims), dma(dims)]
 
-    new_w, new_m, new_f, new_s = pl.pallas_call(
+    parts, gradient = pl.pallas_call(
         kernel,
         out_shape=(
-            jax.ShapeDtypeStruct((NBLK, 128, HD), bf16),
-            jax.ShapeDtypeStruct((2, 128, HD), f32),
-            jax.ShapeDtypeStruct((2, 128, HD), f32),
-            jax.ShapeDtypeStruct((2, 128, HD), f32),
+            jax.ShapeDtypeStruct((8, PAD, SUB, HD), bf16),
+            jax.ShapeDtypeStruct((32, SUB, HD), f32),
         ),
         in_specs=[smem] * 2 + [vmem] * 8,
-        out_specs=(vmem,) * 4,
+        out_specs=(vmem,) * 2,
         scratch_shapes=[
             pltpu.VMEM((HROWS, TOK), bf16),
             pltpu.VMEM((HROWS, TOK), bf16),
-            pltpu.VMEM((2 * HROWS, 128), bf16),
-            pltpu.VMEM((HROWS, 128), bf16),
+            pltpu.VMEM((HROWS, 256), bf16),
+            pltpu.VMEM((HROWS // 2, 256), bf16),
             pltpu.VMEM((CHUNKS, HD, CTOK), f32),
-            pltpu.VMEM((CHUNKS, HD, CTOK), f32),
-            pltpu.VMEM((CHUNKS, HD, CTOK), f32),
+            pltpu.VMEM((CHUNKS, 96, CTOK), i32),
+            pltpu.VMEM((CHUNKS, 96, CTOK), i32),
+            pltpu.VMEM((CHUNKS, 8, CTOK), f32),
+            pltpu.VMEM((CHUNKS, 8, CTOK), f32),
             pltpu.VMEM((TOK, HD), bf16),
             pltpu.VMEM((2, TOK, HD), bf16),
-            pltpu.VMEM((HROWS, HD), f32),
-            pltpu.VMEM((4, NBLK + 1, 8, HD), i32),
-            pltpu.VMEM((4, NBLK + 1, 8, HD), i32),
-            pltpu.VMEM((PAD, SUB, HD), f32),
+            pltpu.VMEM((HROWS + 256, HD), f32),
+            pltpu.VMEM((2, 4, 4 * OWN + 1, 8, HD), i32),
+            pltpu.VMEM((2, 4, 4 * OWN + 1, 8, HD), i32),
+            pltpu.VMEM((4 * OWN, SUB, HD), f32),
             pltpu.VMEM((8, OWN + 1, 8, HD), i32),
             pltpu.VMEM((8, OWN + 1, 8, HD), i32),
             pltpu.VMEM((OWN, SUB, HD), f32),
@@ -523,17 +593,17 @@
             pltpu.VMEM((96, 8, HD), i32),
             pltpu.VMEM((3, 8, OWN, 8, HD), i32),
             pltpu.VMEM((3, PAD, 8, HD), i32),
-            pltpu.VMEM((8, PAD, SUB, HD), bf16),
             pltpu.VMEM((8, 4, SUB, HD), f32),
-            pltpu.VMEM((32, SUB, HD), f32),
         ]
-        + pair(3, CHUNKS)
+        + pair(2, CHUNKS)
+        + pair(2, CHUNKS)
         + pair(CHUNKS)
         + pair(8)
         + pair(CHUNKS)
         + pair(CHUNKS)
+        + pair(CHUNKS)
         + [dma((CHUNKS,)), dma((CHUNKS, 2))]
-        + pair(3)
+        + pair(2, 3)
         + pair(8)
         + pair(7)
         + pair(7)
@@ -552,6 +622,20 @@
         activation.T, w_query.reshape(NBLK, 128, HD), key_rows, value_rows, out_grad,
         master_copy, first_moment, second_moment,
     )
+    new_w, new_m, new_f, new_s = pl.pallas_call(
+        finish,
+        out_shape=(
+            jax.ShapeDtypeStruct((NBLK, 128, HD), bf16),
+            jax.ShapeDtypeStruct((2, 128, HD), f32),
+            jax.ShapeDtypeStruct((2, 128, HD), f32),
+            jax.ShapeDtypeStruct((2, 128, HD), f32),
+        ),
+        in_specs=[smem, anywhere, anywhere] + [vmem] * 3,
+        out_specs=(anywhere, vmem, vmem, vmem),
+        scratch_shapes=[pltpu.VMEM((32, SUB, HD), f32), dma((9,))],
+        compiler_params=pltpu.CompilerParams(vmem_limit_bytes=56 * 2**20),
+        name="finish",
+    )(slot_code, parts.reshape(8, PAD // 2, 2 * SUB, HD), gradient, master_copy, first_moment, second_moment)
     return (new_w.reshape(NBLK * 128, HD), new_m, new_f, new_s)
 
 

time: 145 us -> 187 us (1.29)
  Pallas kernels: 137 us -> 182 us
  local copies, waits for them, and re-layouts: 5.29 us -> 0 us
    pallas_call x1 -> x2, Pallas kernels: 137 us -> 182 us  [the longest x1 128 us: body(): pl.pallas_call(kernel, out_shape=(jax.ShapeDtypeStruct((8, PAD, SUB, HD),...]
    unnamed x10 -> x0, local copies, waits for them, and re-layouts: 4.78 us -> none
where the time goes in v4:
time: 187 us; the launch traced here: 186 us
  Pallas kernels  182 us (97%)
  other arithmetic  2.62 us (1%)
    pallas_call x1, Pallas kernels, body(): pl.pallas_call(kernel, out_shape=(jax.ShapeDtypeStruct((8, PAD, SUB, HD),...  128 us
    pallas_call x1, Pallas kernels, body(): pl.pallas_call(finish, out_shape=(jax.ShapeDtypeStruct((NBLK, 128, HD), b...  54.6 us

profile of v4, /device:TPU:1, one launch (start us, length us, event | category | flops | bytes accessed | tf_op | source)
XLA Modules:
  0.0 185.6 jit_solution(9444013600633896648)
XLA Ops:
  0.6 0.8 convert_reduce_fusion
  1.5 1.2 fusion.10
  2.6 0.6 select_reduce_fusion.slot_code
  3.2 127.8 %project_back.1 = (bf16[8,56,16,128]{3,2,1,0:T(8,128)(2,1)}, f32[32,16,128]{2,1,0:T(8,128)}) custom-call(s32[128]{0:T(128)} %select_reduce_fusion.slot_code, s32[52]{0:T(128)} %get-tuple-element.16.block_code, bf16[832,384]{1,0:T(8,128)(2,1)} %bitcast.9, bf16[52,128,128]{2,1,0:T(8,128)(2,1)} %bitcast.8, bf16[384,128]{1,0:T(8,128)(2,1)} %keys.1, ...), custom_call_target="tpu_custom_call" | custom-call | tf_op jit(solution)/shard_map/project_back/pallas_call | solution.py:564
  131.0 54.6 %finish.1 = (bf16[52,128,128]{2,1,0:T(8,128)(2,1)}, f32[2,128,128]{2,1,0:T(8,128)}, f32[2,128,128]{2,1,0:T(8,128)}, f32[2,128,128]{2,1,0:T(8,128)}) custom-call(s32[128]{0:T(128)} %select_reduce_fusion.slot_code, bf16[8,28,32,128]{3,2,1,0:T(8,128)(2,1)} %bitcast.7, f32[32,16,128]{2,1,0:T(8,128)} %get-tuple-element.11.recv, f32[2,128,128]{2,1,0:T(8,128)} %master.3, ...), custom_call_target="tpu_custom_call" | custom-call | tf_op jit(solution)/shard_map/finish/pallas_call | solution.py:625

commit v5 on v4

--- a/solution.py
+++ b/solution.py
@@ -2,6 +2,7 @@
 
 import jax
 import jax.numpy as jnp
+import numpy as np
 from jax import lax
 from jax.experimental import pallas as pl
 from jax.experimental.pallas import tpu as pltpu
@@ -539,17 +540,22 @@
     activation, w_query, key_rows, value_rows, out_grad, owners, master_copy, first_moment, second_moment
 ):
     own_row = owners[0, :, 0]
-    order = jnp.arange(NBLK, dtype=jnp.int32)
-    earlier = (own_row[:, None] == own_row[None, :]) & (order[:, None] < order[None, :])
-    second_slot = jnp.sum(earlier.astype(jnp.int32), axis=0)
-    target = own_row * 2 + second_slot
-    match = target[None, :] == jnp.arange(128, dtype=jnp.int32)[:, None]
+    order = np.arange(NBLK, dtype=np.int32)
     unit = (order % HALF) * 2
     place = (unit // OWN) * 8 + unit % OWN
     place = place + 64 * (((unit + 1) // OWN) * 8 + (unit + 1) % OWN)
     place = place + 4096 * (order // HALF) + 8192
-    slot_code = jnp.sum(jnp.where(match, place[None, :], 0), axis=1)
-    block_code = (own_row // 8) * (OWN * 128) + (own_row % 8) * 12 + second_slot * 2
+    keyed = jnp.asarray(order * 65536 + place, jnp.int32)
+    slots = np.arange(128, dtype=np.int32)
+    match = own_row[None, :] == jnp.asarray(slots[:, None] >> 1)
+    lowest = jnp.min(jnp.where(match, keyed[None, :], 1 << 30), axis=1)
+    highest = jnp.max(jnp.where(match, keyed[None, :], -1), axis=1)
+    upper = jnp.asarray((slots & 1) == 1)
+    there = jnp.where(upper, highest > lowest, highest >= 0)
+    slot_code = jnp.where(there, jnp.where(upper, highest, lowest) & 65535, 0)
+    earlier = (own_row[:, None] == own_row[None, :]) & jnp.asarray(order[None, :] < order[:, None])
+    second_slot = jnp.sum(earlier.astype(jnp.int32), axis=1)
+    block_code = (own_row >> 3) * (OWN * 128) + (own_row & 7) * 12 + second_slot * 2
     smem = pl.BlockSpec(memory_space=pltpu.SMEM)
     vmem = pl.BlockSpec(memory_space=pltpu.VMEM)
     anywhere = pl.BlockSpec(memory_space=pl.ANY)
@@ -631,7 +637,7 @@
             jax.ShapeDtypeStruct((2, 128, HD), f32),
         ),
         in_specs=[smem, anywhere, anywhere] + [vmem] * 3,
-        out_specs=(anywhere, vmem, vmem, vmem),
+        out_specs=(vmem,) * 4,
         scratch_shapes=[pltpu.VMEM((32, SUB, HD), f32), dma((9,))],
         compiler_params=pltpu.CompilerParams(vmem_limit_bytes=56 * 2**20),
         name="finish",

time: 187 us -> 138 us (0.74)
  Pallas kernels: 182 us -> 132 us
    pallas_call x1, Pallas kernels: 54.6 us -> 3.96 us  [body(): pl.pallas_call(finish, out_shape=(jax.ShapeDtypeStruct((NBLK, 128, HD), b...]
where the time goes in v5:
time: 138 us; the launch traced here: 136 us
  Pallas kernels  132 us (96%)
  other arithmetic  4.05 us (3%)
    pallas_call x1, Pallas kernels, body(): pl.pallas_call(kernel, out_shape=(jax.ShapeDtypeStruct((8, PAD, SUB, HD),...  128 us
    pallas_call x1, Pallas kernels, body(): pl.pallas_call(finish, out_shape=(jax.ShapeDtypeStruct((NBLK, 128, HD), b...  3.96 us

profile of v5, /device:TPU:1, one launch (start us, length us, event | category | flops | bytes accessed | tf_op | source)
XLA Modules:
  0.0 136.5 jit_solution(15021030797743419257)
XLA Ops:
  0.6 0.9 convert_reduce_fusion
  1.5 1.2 multiply_add_fusion.block_code
  2.7 0.8 fusion.1
  3.5 1.2 select_select_fusion.slot_code
  4.7 127.8 %project_back.1 = (bf16[8,56,16,128]{3,2,1,0:T(8,128)(2,1)}, f32[32,16,128]{2,1,0:T(8,128)}) custom-call(s32[128]{0:T(128)} %select_select_fusion.slot_code, s32[52]{0:T(128)} %multiply_add_fusion.block_code, bf16[832,384]{1,0:T(8,128)(2,1)} %bitcast.8, bf16[52,128,128]{2,1,0:T(8,128)(2,1)} %bitcast.7, bf16[384,128]{1,0:T(8,128)(2,1)} %keys.1, ...), custom_call_target="tpu_custom_call" | custom-call | tf_op jit(solution)/shard_map/project_back/pallas_call | solution.py:570
  132.5 4.0 %finish.1 = (bf16[52,128,128]{2,1,0:T(8,128)(2,1)}, f32[2,128,128]{2,1,0:T(8,128)}, f32[2,128,128]{2,1,0:T(8,128)}, f32[2,128,128]{2,1,0:T(8,128)}) custom-call(s32[128]{0:T(128)} %select_select_fusion.slot_code, bf16[8,28,32,128]{3,2,1,0:T(8,128)(2,1)} %bitcast.6, f32[32,16,128]{2,1,0:T(8,128)} %get-tuple-element.11.recv, f32[2,128,128]{2,1,0:T(8,128)} %master.3, ...), custom_call_target="tpu_custom_call" | custom-call | tf_op jit(solution)/shard_map/finish/pallas_call | solution.py:631

commit v6 on v4

--- a/solution.py
+++ b/solution.py
@@ -386,18 +386,17 @@
             cp.wait_recv()
         steps = [step_of(yr[h, p, 4 * OWN, 0:1]) for p in range(4)]
 
-        def add_y(k, top):
+        def add_y(k, carry):
             for j in range(OWN):
                 u = k * OWN + j
                 total = unpack(yr[h, 0, u], steps[0])
                 for p in range(1, 4):
                     total = total + unpack(yr[h, p, u], steps[p])
                 gsum[u] = total
-                top = jnp.maximum(top, jnp.max(jnp.abs(total), axis=0, keepdims=True))
-            return top
-
-        top = lax.fori_loop(0, 4, add_y, jnp.zeros((1, HD), f32))
-        e = jnp.broadcast_to(level(top), (8, HD))
+            return carry
+
+        lax.fori_loop(0, 4, add_y, 0)
+        e = jnp.broadcast_to(level(LEVELS * (steps[0] + steps[1] + steps[2] + steps[3])), (8, HD))
         inv = inverse_of(e[:1])
 
         def to_fixed_z(k, carry):
@@ -427,13 +426,11 @@
     for cp in state_z:
         cp.wait_recv()
     steps = [step_of(zr[z, OWN, 0:1]) for z in range(8)]
-    top = jnp.zeros((1, HD), f32)
     for j in range(OWN):
         total = unpack(zr[0, j], steps[0])
         for z in range(1, 8):
             total = total + unpack(zr[z, j], steps[z])
         red[j] = total
-        top = jnp.maximum(top, jnp.max(jnp.abs(total), axis=0, keepdims=True))
         u = zl * OWN + j
         at = (block_code[jnp.minimum(c * HALF + u // 2, NBLK - 1)] >> 7) + j
         m_state = unpack(szr[0, at], TOP_MASTER / FIXED)
@@ -449,15 +446,18 @@
     for d in range(1, 8):
         z = lax.rem(zl + d, 8)
         w_z.append(go(weights(zl, part), weights(zl, part), w_s.at[d - 1], w_r.at[d - 1], at_z(z)))
-    e = jnp.broadcast_to(level(top), (8, HD))
-    inv = inverse_of(e[:1])
+    bound = steps[0]
+    for z in range(1, 8):
+        bound = bound + steps[z]
+    e = level(LEVELS * bound)
+    inv = inverse_of(e)
+    g_step = step_of(e)
     for j in range(OWN):
-        gq[zl * 8 + j] = pack(red[j], inv)
-    gq[zl * 8 + OWN] = e
+        gq[zl * OWN + j] = pack(red[j], inv)
     g_z = []
     for d in range(1, 8):
         z = lax.rem(zl + d, 8)
-        at = gq.at[pl.ds(zl * 8, 8)]
+        at = gq.at[pl.ds(zl * OWN, OWN)]
         g_z.append(go(at, at, a_s.at[d - 1], a_r.at[d - 1], at_z(z)))
 
     back_y = []
@@ -482,7 +482,7 @@
             code = slot_code[zl * 16 + p * 2 + j]
             for s in range(2):
                 u = (code >> (6 * s)) & 63
-                send_g[p, j * 2 + s] = unpack(gq[u], step_of(gq[u | OWN][:1]))
+                send_g[p, j * 2 + s] = unpack(gq[u], g_step)
     to_owner = []
     for d in range(1, 8):
         p = lax.rem(part + d, 8)
@@ -511,11 +511,10 @@
         cp.wait_send()
 
 
-def finish(slot_code, parts, recv, master, first, second, out_w, out_m, out_f, out_s, recv_g, sem):
+def finish(slot_code, parts, recv, master, first, second, out_w, out_m, out_f, out_s, recv_g, held, sem):
     moves = [pltpu.make_async_copy(recv, recv_g, sem.at[8])]
     for p in range(8):
-        dst = out_w.at[pl.ds((p % 2) * HALF, HALF), pl.ds((p // 2) * 32, 32)]
-        moves.append(pltpu.make_async_copy(parts.at[p, pl.ds(0, HALF)], dst, sem.at[p]))
+        moves.append(pltpu.make_async_copy(parts.at[p], held.at[p], sem.at[p]))
     for cp in moves:
         cp.start()
     moves[0].wait()
@@ -531,8 +530,11 @@
                 out_m[j, r] = nm
                 out_f[j, r] = nf
                 out_s[j, r] = ns
-    for cp in moves[1:]:
-        cp.wait()
+    for p in range(8):
+        moves[1 + p].wait()
+        b = (p % 2) * HALF
+        r = (p // 2) * 32
+        out_w[b : b + HALF, r : r + 32] = held[p, 0:HALF]
 
 
 def body(
@@ -545,11 +547,11 @@
     target = own_row * 2 + second_slot
     match = target[None, :] == jnp.arange(128, dtype=jnp.int32)[:, None]
     unit = (order % HALF) * 2
-    place = (unit // OWN) * 8 + unit % OWN
-    place = place + 64 * (((unit + 1) // OWN) * 8 + (unit + 1) % OWN)
+    place = unit
+    place = place + 64 * (unit + 1)
     place = place + 4096 * (order // HALF) + 8192
     slot_code = jnp.sum(jnp.where(match, place[None, :], 0), axis=1)
-    block_code = (own_row // 8) * (OWN * 128) + (own_row % 8) * 12 + second_slot * 2
+    block_code = (own_row >> 3) * (OWN * 128) + (own_row & 7) * 12 + second_slot * 2
     smem = pl.BlockSpec(memory_space=pltpu.SMEM)
     vmem = pl.BlockSpec(memory_space=pltpu.VMEM)
     anywhere = pl.BlockSpec(memory_space=pl.ANY)
@@ -588,7 +590,7 @@
             pltpu.VMEM((8, OWN + 1, 8, HD), i32),
             pltpu.VMEM((8, OWN + 1, 8, HD), i32),
             pltpu.VMEM((OWN, SUB, HD), f32),
-            pltpu.VMEM((64, 8, HD), i32),
+            pltpu.VMEM((PAD, 8, HD), i32),
             pltpu.VMEM((8, 12, 8, HD), i32),
             pltpu.VMEM((96, 8, HD), i32),
             pltpu.VMEM((3, 8, OWN, 8, HD), i32),
@@ -631,8 +633,12 @@
             jax.ShapeDtypeStruct((2, 128, HD), f32),
         ),
         in_specs=[smem, anywhere, anywhere] + [vmem] * 3,
-        out_specs=(anywhere, vmem, vmem, vmem),
-        scratch_shapes=[pltpu.VMEM((32, SUB, HD), f32), dma((9,))],
+        out_specs=(vmem,) * 4,
+        scratch_shapes=[
+            pltpu.VMEM((32, SUB, HD), f32),
+            pltpu.VMEM((8, PAD // 2, 2 * SUB, HD), bf16),
+            dma((9,)),
+        ],
         compiler_params=pltpu.CompilerParams(vmem_limit_bytes=56 * 2**20),
         name="finish",
     )(slot_code, parts.reshape(8, PAD // 2, 2 * SUB, HD), gradient, master_copy, first_moment, second_moment)

time: 187 us -> 136 us (0.73)
  Pallas kernels: 182 us -> 132 us
    pallas_call x1, Pallas kernels: 54.6 us -> 4.02 us  [body(): pl.pallas_call(finish, out_shape=(jax.ShapeDtypeStruct((NBLK, 128, HD), b...]
where the time goes in v6:
time: 136 us; the launch traced here: 135 us
  Pallas kernels  132 us (97%)
  other arithmetic  2.61 us (2%)
    pallas_call x1, Pallas kernels, body(): pl.pallas_call(kernel, out_shape=(jax.ShapeDtypeStruct((8, PAD, SUB, HD),...  128 us
    pallas_call x1, Pallas kernels, body(): pl.pallas_call(finish, out_shape=(jax.ShapeDtypeStruct((NBLK, 128, HD), b...  4.02 us

profile of v6, /device:TPU:1, one launch (start us, length us, event | category | flops | bytes accessed | tf_op | source)
XLA Modules:
  0.0 134.9 jit_solution(2356060147463567347)
XLA Ops:
  0.6 0.8 convert_reduce_fusion
  1.5 1.2 multiply_add_fusion
  2.6 0.6 select_reduce_fusion.slot_code
  3.2 127.6 %project_back.1 = (bf16[8,56,16,128]{3,2,1,0:T(8,128)(2,1)}, f32[32,16,128]{2,1,0:T(8,128)}) custom-call(s32[128]{0:T(128)} %select_reduce_fusion.slot_code, s32[52]{0:T(128)} %get-tuple-element.16.block_code, bf16[832,384]{1,0:T(8,128)(2,1)} %bitcast.9, bf16[52,128,128]{2,1,0:T(8,128)(2,1)} %bitcast.8, bf16[384,128]{1,0:T(8,128)(2,1)} %keys.1, ...), custom_call_target="tpu_custom_call" | custom-call | tf_op jit(solution)/shard_map/project_back/pallas_call | solution.py:566
  130.9 4.0 %finish.1 = (bf16[52,128,128]{2,1,0:T(8,128)(2,1)}, f32[2,128,128]{2,1,0:T(8,128)}, f32[2,128,128]{2,1,0:T(8,128)}, f32[2,128,128]{2,1,0:T(8,128)}) custom-call(s32[128]{0:T(128)} %select_reduce_fusion.slot_code, bf16[8,28,32,128]{3,2,1,0:T(8,128)(2,1)} %bitcast.7, f32[32,16,128]{2,1,0:T(8,128)} %get-tuple-element.11.recv, f32[2,128,128]{2,1,0:T(8,128)} %master.3, ...), custom_call_target="tpu_custom_call" | custom-call | tf_op jit(solution)/shard_map/finish/pallas_call | solution.py:627

commit v7 on v6

--- a/solution.py
+++ b/solution.py
@@ -99,7 +99,7 @@
     wst, recv_g,
     whole, sib, wt, wo, qo, po, pr, pm, pn, dqs, dqa, grad, ys, yr, gsum, zs, zr, red, gq,
     sys, syr, szs, szr, send_g,
-    x_s, x_r, f_s, f_r, s_s, s_r, b_s, b_r, q_s, q_r, n_s, n_r, h_s, h_r, d_s, d_r, y_s, y_r, r_s, r_r,
+    x_s, x_r, f_s, f_r, s_s, s_r, b_s, b_r, e_s, e_r, q_s, q_r, n_s, n_r, h_s, h_r, d_s, d_r, y_s, y_r, r_s, r_r,
     a_s, a_r, o_s, o_r, w_s, w_r, v_s, v_r, c_s, c_r, k_s, k_r, p_s, p_r, l_sem,
 ):
     dp = lax.axis_index("dp")
@@ -173,8 +173,10 @@
         return cp
 
     eighth = rows(part * 208, 208, 16)
+    odd = lax.rem(zl, 2)
+    lanes = [rows(odd * 128, 128, 128), rows((1 - odd) * 128, 128, 128)]
     w_cross = go(
-        wt.at[rows((1 - a) * (HROWS // 2) + part * 208, 208, 16)], wo.at[eighth],
+        wt.at[rows((1 - a) * (HROWS // 2) + part * 208, 208, 16), lanes[0]], wo.at[eighth, lanes[0]],
         b_s.at[0], b_r.at[0], opposite,
     )
 
@@ -235,12 +237,20 @@
     send_states(0)
     send_states(1)
     pass_on(2)
+    w_cross.wait_recv()
+    at = wo.at[eighth, lanes[0]]
+    w_next = go(at, at, e_s.at[0], e_r.at[0], at_z(zl + 1 - 2 * odd))
+    w_part = []
+
+    def spread(n, ss, rs):
+        at = wo.at[eighth, lanes[n]]
+        for d in range(1, 8):
+            w_part.append(go(at, at, ss.at[d], rs.at[d], at_part(lax.rem(part + d, 8))))
+
+    spread(0, b_s, b_r)
+    w_next.wait_recv()
+    spread(1, e_s, e_r)
     pass_on(1)
-    w_cross.wait_recv()
-    w_part = []
-    for d in range(1, 8):
-        p = lax.rem(part + d, 8)
-        w_part.append(go(wo.at[eighth], wo.at[eighth], b_s.at[d], b_r.at[d], at_part(p)))
     pass_on(0)
 
     def partial(weights, first_row, i):
@@ -600,6 +610,7 @@
         + pair(2, CHUNKS)
         + pair(2, CHUNKS)
         + pair(CHUNKS)
+        + pair(8)
         + pair(8)
         + pair(CHUNKS)
         + pair(CHUNKS)

time: 136 us -> 134 us (0.985)
  no operation moved by 1% of the time
where the time goes in v7:
time: 134 us
  Pallas kernels  131 us (98%)
  other arithmetic  2.61 us (2%)
    pallas_call x1, Pallas kernels, body(): pl.pallas_call(kernel, out_shape=(jax.ShapeDtypeStruct((8, PAD, SUB, HD),...  127 us
    pallas_call x1, Pallas kernels, body(): pl.pallas_call(finish, out_shape=(jax.ShapeDtypeStruct((NBLK, 128, HD), b...  4.02 us

profile of v7, /device:TPU:1, one launch (start us, length us, event | category | flops | bytes accessed | tf_op | source)
XLA Modules:
  0.0 134.1 jit_solution(2965823313677732092)
XLA Ops:
  0.6 0.8 convert_reduce_fusion
  1.5 1.2 multiply_add_fusion
  2.6 0.6 select_reduce_fusion.slot_code
  3.2 126.8 %project_back.1 = (bf16[8,56,16,128]{3,2,1,0:T(8,128)(2,1)}, f32[32,16,128]{2,1,0:T(8,128)}) custom-call(s32[128]{0:T(128)} %select_reduce_fusion.slot_code, s32[52]{0:T(128)} %get-tuple-element.16.block_code, bf16[832,384]{1,0:T(8,128)(2,1)} %bitcast.9, bf16[52,128,128]{2,1,0:T(8,128)(2,1)} %bitcast.8, bf16[384,128]{1,0:T(8,128)(2,1)} %keys.1, ...), custom_call_target="tpu_custom_call" | custom-call | tf_op jit(solution)/shard_map/project_back/pallas_call | solution.py:576
  130.1 4.0 %finish.1 = (bf16[52,128,128]{2,1,0:T(8,128)(2,1)}, f32[2,128,128]{2,1,0:T(8,128)}, f32[2,128,128]{2,1,0:T(8,128)}, f32[2,128,128]{2,1,0:T(8,128)}) custom-call(s32[128]{0:T(128)} %select_reduce_fusion.slot_code, bf16[8,28,32,128]{3,2,1,0:T(8,128)(2,1)} %bitcast.7, f32[32,16,128]{2,1,0:T(8,128)} %get-tuple-element.11.recv, f32[2,128,128]{2,1,0:T(8,128)} %master.3, ...), custom_call_target="tpu_custom_call" | custom-call | tf_op jit(solution)/shard_map/finish/pallas_call | solution.py:638
